TPU v7x, 32 devices: a whole 2x2x4 slice. The times are simulated.
32 devices in a mesh: gz: 4 (over x, core), ma: 8 (over z, y).
Axes of the slice: x: 2, y: 2, z: 4, core: 2. Of those that a mesh axis runs over, the one named last changes fastest.
Arguments:
- forward: float32 [4, 2, 1024, 4096], P('gz', None, 'ma'), may hold values from -6 to 6
- cotangent: float32 [4, 2, 1024, 4096], P('gz', None, 'ma'), may hold values from -6 to 6
- mode_order: int32 [1024], replicated, may hold values from 0 to 1023, each once
- region: int32 [128, 128], replicated, may hold values from 0 to 7
- chi: float32 [8], replicated, may hold values from 0.5 to 2
- phase: float32 [1024, 4096], P('ma'), may hold values from -3.140625 to 3.140625
- loss: float32 [4, 1024], P('gz', 'ma'), may hold values from 0.5 to 1
Outputs:
- adjoint: float32 [4, 2, 1024, 4096], P('gz', None, 'ma')
Inputs may be any that keep to these rules, and one draw needn't show every extreme that they name: Each number appears once; stored mode m has order mode_order[m] // 32 along the first transverse coordinate and mode_order[m] % 32 along the second.
All inputs are finite; a program needn't handle non-finite values.
Results may differ from a plain program's by a relative error of at most 0.0003.
Values sent between devices are 32-bit elements; how exact they have to be, the bound alone decides.
A program may use at most 320 MiB of HBM per device.

v0:
```python
import math

import jax
import jax.numpy as jnp
from jax import lax
from jax.sharding import PartitionSpec as P

HG_ORDER = 32
MODES = 1024
GRID = 128
REGIONS = 8


gamma_kerr = 2.0
half_width = 10.0


def prefix(shard, axis, combine, identity):
    devices, mine = (lax.axis_size(axis), lax.axis_index(axis))
    everything = jax.tree.map(lambda part: lax.all_gather(part, axis), shard)
    start = jax.tree.map(
        lambda part, zero: jnp.broadcast_to(jnp.asarray(zero, part.dtype), part.shape),
        shard,
        identity,
    )

    def turn(k, before):
        at = devices - 1 - k
        reached = at > mine
        new = combine(before, jax.tree.map(lambda part: part[at], everything))
        return jax.tree.map(lambda a, b: jnp.where(reached, a, b), new, before)

    return lax.fori_loop(0, devices, turn, start)


def hermite_table(grid_points, degrees):
    spacing = 2.0 * half_width / grid_points
    coords = (jnp.arange(grid_points, dtype=jnp.float32) - (grid_points - 1) / 2.0) * spacing
    columns = [jnp.exp(-0.5 * coords * coords) * math.pi ** (-0.25)]
    columns.append(math.sqrt(2.0) * coords * columns[0])
    for degree in range(2, degrees):
        following = (
            math.sqrt(2.0 / degree) * coords * columns[degree - 1]
            - math.sqrt((degree - 1.0) / degree) * columns[degree - 2]
        )
        columns.append(following)
    return jnp.stack(columns, axis=1) * math.sqrt(spacing)


def modes_to_grid(fields, table):
    partial_grid = jnp.einsum("...pqt,yq->...pyt", fields, table, precision=lax.Precision.HIGHEST)
    return jnp.einsum("...pyt,xp->...xyt", partial_grid, table, precision=lax.Precision.HIGHEST)


def grid_to_modes(values, table):
    partial_grid = jnp.einsum("...xyt,xp->...pyt", values, table, precision=lax.Precision.HIGHEST)
    return jnp.einsum("...pyt,yq->...pqt", partial_grid, table, precision=lax.Precision.HIGHEST)


def kerr_adjoint(forward, cotangent, table, chi_grid, inverse, mode_order):
    leading = forward.shape[:-2]
    samples = forward.shape[-1]
    degrees = table.shape[1]

    def ordered_grid(fields):
        ordered = jnp.take(fields, inverse, axis=-2)
        return ordered.reshape(leading + (degrees, degrees, samples))

    field_grid = modes_to_grid(ordered_grid(forward), table)
    cot_grid = modes_to_grid(ordered_grid(cotangent), table)
    field_real = field_grid[..., 0, :, :, :]
    field_imag = field_grid[..., 1, :, :, :]
    cot_real = cot_grid[..., 0, :, :, :]
    cot_imag = cot_grid[..., 1, :, :, :]
    strength = gamma_kerr * chi_grid[:, :, None]
    intensity = field_real * field_real + field_imag * field_imag
    cross = 2.0 * field_real * field_imag
    grad_real = strength * (
        -cross * cot_real + (intensity + 2.0 * field_real * field_real) * cot_imag
    )
    grad_imag = strength * (
        -(intensity + 2.0 * field_imag * field_imag) * cot_real + cross * cot_imag
    )
    projected = grid_to_modes(jnp.stack([grad_real, grad_imag], axis=-4), table)
    flat = projected.reshape(leading + (degrees * degrees, samples))
    return jnp.take(flat, mode_order, axis=-2)


def complex_product(spec, left_pair, right_pair):
    real_out = jnp.einsum(
        spec, left_pair[0], right_pair[0], precision=lax.Precision.HIGHEST
    ) - jnp.einsum(spec, left_pair[1], right_pair[1], precision=lax.Precision.HIGHEST)
    imag_out = jnp.einsum(
        spec, left_pair[0], right_pair[1], precision=lax.Precision.HIGHEST
    ) + jnp.einsum(spec, left_pair[1], right_pair[0], precision=lax.Precision.HIGHEST)
    return (real_out, imag_out)


def complex_scale(left_pair, right_pair):
    return (
        left_pair[0] * right_pair[0] - left_pair[1] * right_pair[1],
        left_pair[0] * right_pair[1] + left_pair[1] * right_pair[0],
    )


def adjoint_dispersion(source, phase):
    points = source.shape[0]
    modes = source.shape[2]
    length = source.shape[3]
    inner_size = 128
    outer_size = length // inner_size
    first_index = jnp.arange(outer_size, dtype=jnp.int32)
    second_index = jnp.arange(inner_size, dtype=jnp.int32)
    first_angle = (
        2.0
        * math.pi
        / outer_size
        * (first_index[:, None] * first_index[None, :] % outer_size).astype(jnp.float32)
    )
    twiddle_angle = (
        2.0
        * math.pi
        / length
        * (first_index[:, None] * second_index[None, :] % length).astype(jnp.float32)
    )
    second_angle = (
        2.0
        * math.pi
        / inner_size
        * (second_index[:, None] * second_index[None, :] % inner_size).astype(jnp.float32)
    )
    first_fwd = (jnp.cos(first_angle), -jnp.sin(first_angle))
    first_back = (jnp.cos(first_angle), jnp.sin(first_angle))
    twiddle_fwd = (jnp.cos(twiddle_angle), -jnp.sin(twiddle_angle))
    twiddle_back = (jnp.cos(twiddle_angle), jnp.sin(twiddle_angle))
    second_fwd = (jnp.cos(second_angle), -jnp.sin(second_angle))
    second_back = (jnp.cos(second_angle), jnp.sin(second_angle))
    signal = (
        source[:, 0].reshape(points, modes, outer_size, inner_size),
        source[:, 1].reshape(points, modes, outer_size, inner_size),
    )
    segmented = complex_product("zmab,ak->zmkb", signal, first_fwd)
    segmented = complex_scale(segmented, twiddle_fwd)
    spectrum = complex_product("zmkb,bj->zmkj", segmented, second_fwd)
    turned = phase.reshape(modes, inner_size, outer_size).transpose(0, 2, 1)
    spectrum = complex_scale(spectrum, (jnp.cos(turned), -jnp.sin(turned)))
    segmented = complex_product("zmkj,bj->zmkb", spectrum, second_back)
    segmented = complex_scale(segmented, twiddle_back)
    signal = complex_product("zmkb,ak->zmab", segmented, first_back)
    factor = 1.0 / length
    return (
        jnp.stack(
            [signal[0].reshape(points, modes, length), signal[1].reshape(points, modes, length)],
            axis=1,
        )
        * factor
    )


def affine_combine(former, latter):
    return (latter[0] * former[0], latter[1] + latter[0][None, :, None] * former[1])


def on_device(forward, cotangent, mode_order, region, chi, phase, loss):
    groups = lax.axis_size("ma")
    points = forward.shape[0]
    local_modes = forward.shape[2]
    time_points = forward.shape[3]
    block_size = time_points // groups
    table = hermite_table(GRID, HG_ORDER)
    matches = (region[:, :, None] == jnp.arange(REGIONS, dtype=jnp.int32)[None, None, :]).astype(
        jnp.float32
    )
    chi_grid = jnp.sum(matches * chi[None, None, :], axis=-1)
    inverse = jnp.zeros((MODES,), jnp.int32).at[mode_order].set(jnp.arange(MODES, dtype=jnp.int32))
    shaped_forward = forward.reshape(points, 2, local_modes, groups, block_size)
    shaped_cot = cotangent.reshape(points, 2, local_modes, groups, block_size)
    forward_all = lax.all_to_all(shaped_forward, "ma", split_axis=3, concat_axis=2, tiled=True)[
        :, :, :, 0, :
    ]
    cot_all = lax.all_to_all(shaped_cot, "ma", split_axis=3, concat_axis=2, tiled=True)[
        :, :, :, 0, :
    ]
    result = kerr_adjoint(forward_all, cot_all, table, chi_grid, inverse, mode_order)
    kerr = lax.all_to_all(result[:, :, :, None, :], "ma", split_axis=2, concat_axis=3, tiled=True)
    kerr = kerr.reshape(points, 2, local_modes, time_points)
    source = cotangent + kerr
    dispersed = adjoint_dispersion(source, phase)
    partial_value = [None] * points
    factors = [None] * points
    running = dispersed[points - 1]
    product = loss[points - 1]
    partial_value[points - 1] = running
    factors[points - 1] = product
    total_factor = factors[0]
    first_value = partial_value[0]
    scanned = prefix(
        (total_factor, first_value),
        "gz",
        affine_combine,
        (jnp.ones_like(total_factor), jnp.zeros_like(first_value)),
    )
    incoming = scanned[1]
    return jnp.stack([partial_value[0] + factors[0][None, :, None] * incoming], axis=0)


def solution(mesh):
    in_specs = (
        P("gz", None, "ma", None),
        P("gz", None, "ma", None),
        P(),
        P(),
        P(),
        P("ma", None),
        P("gz", "ma"),
    )
    out_specs = P("gz", None, "ma", None)
    return jax.shard_map(
        on_device, mesh=mesh, in_specs=in_specs, out_specs=out_specs, check_vma=False
    )
```

profile of v0, /device:TPU:0, one launch (start us, length us, event | category | flops | bytes accessed | tf_op | source)
XLA Modules:
  0.0 873.2 jit_solution(8973155575599296847)
XLA Ops:
  16.7 7.3 all-to-all-start
  34.2 83.1 %all-to-all-done = f32[1,2,128,8,512]{2,4,1,0,3:T(8,128)} async-done(((f32[1,2,128,8,512]{2,4,1,0,3:T(8,128)}), f32[1,2,128,8,512]{2,4,1,0,3:T(8,128)}, u32[]{:S(2)}, u32[]{:S(2)}) %all-to-all-start) | async-done | bytes 4194336 | tf_op jit(solution)/shard_map/all_to_all | solution.py:178
  134.6 7.4 copy.196
  142.0 72.4 %all-to-all-done.1 = f32[1,2,128,8,512]{2,4,1,0,3:T(8,128)} async-done(((f32[1,2,128,8,512]{2,4,1,0,3:T(8,128)}), f32[1,2,128,8,512]{2,4,1,0,3:T(8,128)}, u32[]{:S(2)}, u32[]{:S(2)}) %all-to-all-start.1) | async-done | bytes 4194336 | tf_op jit(solution)/shard_map/all_to_all | solution.py:181
  219.8 7.4 copy.195
  227.2 13.7 %gather_fusion = f32[1024,2,512]{2,1,0:T(2,128)} fusion(f32[2,1024,512]{2,0,1:T(2,128)} %bitcast.258, s32[1024]{0:T(1024)S(1)} %fusion.138), kind=kCustom, calls=%fused_computation.clone | custom fusion | bytes 8392704 | tf_op jit(solution)/shard_map/jit(_take)/gather | solution.py:66
  240.9 13.9 %gather_fusion.1 = f32[1024,2,512]{2,1,0:T(2,128)} fusion(f32[2,1024,512]{2,0,1:T(2,128)} %bitcast.259, s32[1024]{0:T(1024)S(1)} %fusion.138), kind=kCustom, calls=%fused_computation.1.clone | custom fusion | bytes 8392704 | tf_op jit(solution)/shard_map/jit(_take)/gather | solution.py:66
  254.7 7.3 bitcast_select_fusion.2
  262.1 13.7 %convolution_bitcast_fusion.2 = f32[2,32,128,512]{3,2,1,0:T(8,128)S(1)} fusion(f32[2,32,32,512]{3,0,2,1:T(2,128)S(1)} %bitcast.249, f32[128,32]{0,1:T(8,128)S(1)} %stack.18), kind=kOutput, calls=%fused_computation.31 | convolution fusion | flops 1610616832 | bytes 20987904 | tf_op jit(solution)/shard_map/...pqt,yq->...pyt/dot_general | solution.py:51
  275.8 59.2 %convolution_bitcast_fusion = f32[1,2,128,128,512]{4,2,3,1,0:T(8,128)} fusion(f32[2,32,128,512]{3,2,1,0:T(8,128)S(1)} %convolution_bitcast_fusion.2, f32[128,32]{0,1:T(8,128)S(1)} %stack.18), kind=kOutput, calls=%fused_computation.24 | convolution fusion | flops 6442455040 | bytes 83902464 | tf_op jit(solution)/shard_map/...pyt,xp->...xyt/dot_general | solution.py:52
  335.0 13.7 %convolution_bitcast_fusion.3 = f32[2,32,128,512]{3,2,1,0:T(8,128)S(1)} fusion(f32[2,32,32,512]{3,0,2,1:T(2,128)S(1)} %bitcast.248, f32[128,32]{0,1:T(8,128)S(1)} %stack.18), kind=kOutput, calls=%fused_computation.32 | convolution fusion | flops 1610616832 | bytes 20987904 | tf_op jit(solution)/shard_map/...pqt,yq->...pyt/dot_general | solution.py:51
  348.7 58.8 %convolution_bitcast_fusion.1 = f32[1,2,128,128,512]{4,2,3,1,0:T(8,128)} fusion(f32[2,32,128,512]{3,2,1,0:T(8,128)S(1)} %convolution_bitcast_fusion.3, f32[128,32]{0,1:T(8,128)S(1)} %stack.18), kind=kOutput, calls=%fused_computation.25 | convolution fusion | flops 6442455040 | bytes 83902464 | tf_op jit(solution)/shard_map/...pyt,xp->...xyt/dot_general | solution.py:52
  407.6 64.9 %fusion.7 = (f32[1,1,128,128,512]{4,2,3,1,0:T(8,128)}, f32[1,1,128,128,512]{4,2,3,1,0:T(8,128)}) fusion(f32[1,2,128,128,512]{4,2,3,1,0:T(8,128)} %convolution_bitcast_fusion, f32[1,2,128,128,512]{4,2,3,1,0:T(8,128)} %convolution_bitcast_fusion.1, f32[128,128]{0,1:T(8,128)S(1)} %copy.110), kind=kLoop, calls=%fused_computation.17 | loop fusion | flops 167772160 | bytes 201392128 | tf_op jit(solution)/shard_map/mul | solution.py:78
  472.4 39.9 %fusion.17 = f32[2,32,128,512]{3,1,2,0:T(8,128)S(1)} fusion(f32[1,1,128,128,512]{4,2,3,1,0:T(8,128)} %get-tuple-element.168, f32[1,1,128,128,512]{4,2,3,1,0:T(8,128)} %get-tuple-element.167, f32[128,32]{0,1:T(8,128)S(1)} %stack.18), kind=kOutput, calls=%fused_computation.30 | convolution fusion | flops 6459232256 | bytes 83902464 | tf_op jit(solution)/shard_map/...xyt,xp->...pyt/dot_general | solution.py:56
  512.3 18.2 %fusion.13 = f32[32,2,32,512]{3,0,2,1:T(8,128)S(1)} fusion(f32[2,32,128,512]{3,1,2,0:T(8,128)S(1)} %fusion.17, f32[128,32]{0,1:T(8,128)S(1)} %stack.18), kind=kOutput, calls=%fused_computation.26 | convolution fusion | flops 1610616832 | bytes 20987904 | tf_op jit(solution)/shard_map/...pyt,yq->...pqt/dot_general | solution.py:57
  535.8 13.8 %gather_fusion.2 = f32[1024,2,512]{2,1,0:T(2,128)} fusion(f32[2,1024,512]{2,0,1:T(2,128)} %bitcast.260, s32[1024]{0:T(1024)S(1)} %copy-done.5), kind=kCustom, calls=%fused_computation.2.clone | custom fusion | bytes 8392704 | tf_op jit(solution)/shard_map/jit(_take)/gather | solution.py:86
  549.6 6.6 fusion.20
  562.8 8.3 fusion.213
  576.2 77.1 %all-to-all-done.2 = f32[1,2,1024,1,512]{4,1,3,0,2:T(2,128)} async-done(((f32[1,2,1024,1,512]{4,1,3,0,2:T(2,128)}), f32[1,2,1024,1,512]{4,1,3,0,2:T(2,128)}, u32[]{:S(2)}, u32[]{:S(2)}) %all-to-all-start.2) | async-done | bytes 4194336 | tf_op jit(solution)/shard_map/all_to_all | solution.py:185
  653.3 6.6 copy.126
  740.4 94.7 %all-gather.3.cloned.1.call-done = f32[4,2,128,4096]{3,2,1,0:T(8,128)} async-done(((f32[1,2,128,4096]{3,2,1,0:T(8,128)}), f32[4,2,128,4096]{3,2,1,0:T(8,128)}) %all-gather.3.cloned.1.call-update) | async-done | bytes 16777232 | tf_op jit(solution)/shard_map/all_gather | solution.py:20
  835.2 25.3 %while.16 = (s32[]{:T(128)}, f32[2,128,4096]{2,1,0:T(8,128)}, s32[]{:T(128)}, f32[4,2,128,4096]{3,2,1,0:T(8,128)}, f32[4,128]{1,0:T(4,128)S(1)}, /*index=5*/s32[]{:T(128)}, s32[]{:T(128)}, s32[]{:T(128)}, s32[]{:T(128)}) while((s32[]{:T(128)}, f32[2,128,4096]{2,1,0:T(8,128)}, s32[]{:T(128)}, f32[4,2,128,4096]{3,2,1,0:T(8,128)}, ...), condition=%wide.region_3.5_spmd.clone, body=%wide.region_2.0_spmd.clone.sunk | while | flops 4194312 | bytes 12584615 | solution.py:33
  840.7 6.6 fusion.231
  847.3 6.6 fusion.231
  (97 shorter events, 157.9 us)
Async XLA Ops:
  16.7 100.6 %all-to-all-start = ((f32[1,2,128,8,512]{2,4,1,0,3:T(8,128)}), f32[1,2,128,8,512]{2,4,1,0,3:T(8,128)}, u32[]{:S(2)}, u32[]{:S(2)}) async-start(f32[1,2,128,8,512]{2,4,1,0,3:T(8,128)} %copy.112), calls=%async_computation | async-start | bytes 8388608 | tf_op jit(solution)/shard_map/all_to_all | solution.py:178
  34.2 87.7 %copy-start.4 = (s32[128,128]{1,0:T(8,128)S(1)}, s32[128,128]{1,0:T(8,128)}, u32[]{:S(2)}) copy-start(s32[128,128]{1,0:T(8,128)} %param.14) | copy-start | bytes 196612
  34.2 87.7 %copy-start.9 = (f32[8]{0:T(128)S(1)}, f32[8]{0:T(128)}, u32[]{:S(2)}) copy-start(f32[8]{0:T(128)} %param.15) | copy-start | bytes 100
  34.2 88.2 %copy-start.6 = (s32[1024]{0:T(1024)S(1)}, s32[1024]{0:T(1024)}, u32[]{:S(2)}) copy-start(s32[1024]{0:T(1024)} %param.13) | copy-start | bytes 12292
  117.3 97.1 %all-to-all-start.1 = ((f32[1,2,128,8,512]{2,4,1,0,3:T(8,128)}), f32[1,2,128,8,512]{2,4,1,0,3:T(8,128)}, u32[]{:S(2)}, u32[]{:S(2)}) async-start(f32[1,2,128,8,512]{2,4,1,0,3:T(8,128)} %copy.118), calls=%async_computation.1 | async-start | bytes 8388608 | tf_op jit(solution)/shard_map/all_to_all | solution.py:181
  530.5 5.3 copy-start.5
  535.8 13.8 %copy-start.7 = (pred[1024]{0:T(1024)(128)(4,1)S(1)}, pred[1024]{0:T(1024)(128)(4,1)}, u32[]{:S(2)}) copy-start(pred[1024]{0:T(1024)(128)(4,1)} %compare_and_fusion) | copy-start | bytes 3076
  556.2 97.1 %all-to-all-start.2 = ((f32[1,2,1024,1,512]{4,1,3,0,2:T(2,128)}), f32[1,2,1024,1,512]{4,1,3,0,2:T(2,128)}, u32[]{:S(2)}, u32[]{:S(2)}) async-start(f32[1,2,1024,1,512]{4,1,3,0,2:T(2,128)} %fusion.20), calls=%async_computation.2 | async-start | bytes 8388608 | tf_op jit(solution)/shard_map/all_to_all | solution.py:185
  560.8 274.4 %all-gather.3.cloned.1.call-start = ((), (), s32[]{:S(2)}) async-start(), calls=%async_computation.3 | async-start | bytes 20971520 | tf_op jit(solution)/shard_map/all_gather | solution.py:20
  686.0 3.6 copy-start.2
  723.2 2.9 copy-start.3
  730.0 0.7 copy-start.8
  730.0 5.7 copy-start
  835.2 25.3 %copy-start.1 = (f32[1,128,4096]{2,1,0:T(8,128)S(1)}, f32[1,128,4096]{2,1,0:T(8,128)}, u32[]{:S(2)}) copy-start(f32[1,128,4096]{2,1,0:T(8,128)} %stack.20) | copy-start | bytes 6291460
Sparse Core Ops, SparseCore 0:
  730.2 104.9 all-gather.2
where the time goes:
time: 877 us; the launch traced here: 873 us
  waiting for transfers between devices  327 us (37%)
  matrix products  253 us (29%)
  local copies, waits for them, and re-layouts  129 us (15%)
  other arithmetic  128 us (15%)
  starting transfers between devices  16.5 us (2%)
  between operations  14 us (2%)
    dot_general x2, matrix products, modes_to_grid(): jnp.einsum('...pyt,xp->...xyt', partial_grid, table, precision=lax.Precis...  118 us
    all_gather x1, waiting for transfers between devices, prefix(): everything = jax.tree.map(lambda part: lax.all_gather(part, axis), shard)  94.7 us
    all_to_all x1, waiting for transfers between devices, on_device(): lax.all_to_all(shaped_forward, 'ma', split_axis=3, concat_axis=2, tiled=T...  83.1 us
    all_to_all x1, waiting for transfers between devices, on_device(): lax.all_to_all(result[:, :, :, None, :], 'ma', split_axis=2, concat_axis=...  77.1 us
    all_to_all x1, waiting for transfers between devices, on_device(): lax.all_to_all(shaped_cot, 'ma', split_axis=3, concat_axis=2, tiled=True)  72.4 us
    mul x1, other arithmetic, kerr_adjoint(): strength * (-cross * cot_real + (intensity + 2.0 * field_real * field_rea...  64.9 us
    dot_general x1, matrix products, grid_to_modes(): jnp.einsum('...xyt,xp->...pyt', values, table, precision=lax.Precision.HI...  39.9 us
    gather x2, local copies, waits for them, and re-layouts, ordered_grid(): ordered = jnp.take(fields, inverse, axis=-2)  27.6 us
  transfers between devices with their start and end apart: 4, of which 4 were waited for; matrix products, arithmetic and copies ran while one was open for 6% of the time, Pallas kernels for 0%

commit v1 on v0

v1 whole, which is shorter than its diff:
```python
import functools
import math

import jax
import jax.numpy as jnp
import ml_dtypes
import numpy as np
from jax import lax
from jax.experimental import pallas as pl
from jax.experimental.pallas import tpu as pltpu
from jax.sharding import PartitionSpec as P

HG_ORDER = 32
GRID = 128
REGIONS = 8
LANES = 128
GROUP = 8

gamma_kerr = 2.0
half_width = 10.0

f32 = jnp.float32
bf16 = jnp.bfloat16


def hermite_table(grid_points, degrees):
    spacing = 2.0 * half_width / grid_points
    coords = (np.arange(grid_points, dtype=np.float64) - (grid_points - 1) / 2.0) * spacing
    columns = [np.exp(-0.5 * coords * coords) * math.pi ** (-0.25)]
    columns.append(math.sqrt(2.0) * coords * columns[0])
    for degree in range(2, degrees):
        columns.append(
            math.sqrt(2.0 / degree) * coords * columns[degree - 1]
            - math.sqrt((degree - 1.0) / degree) * columns[degree - 2]
        )
    return (np.stack(columns, axis=1) * math.sqrt(spacing)).astype(np.float32)


def host_parts(array):
    array = np.asarray(array, np.float32)
    high = array.astype(ml_dtypes.bfloat16)
    low = (array - high.astype(np.float32)).astype(ml_dtypes.bfloat16)
    return high, low


def parts(value):
    high = value.astype(bf16)
    low = (value - high.astype(f32)).astype(bf16)
    return high, low


def mm(left, right):
    return jnp.dot(left, right, preferred_element_type=f32)


def kerr_constants():
    table = hermite_table(GRID, HG_ORDER)
    eye = np.eye(GROUP, dtype=np.float32)
    spread = np.einsum("yq,ab->yabq", table, eye).reshape(GRID * GROUP, GROUP * HG_ORDER)
    gather = np.einsum("yq,ab->aqyb", table, eye).reshape(GROUP * HG_ORDER, GRID * GROUP)
    spread_high, spread_low = host_parts(spread)
    gather_high, gather_low = host_parts(gather)
    table_high, table_low = host_parts(table)
    return (
        np.concatenate([spread_high, spread_high, spread_low], axis=1),
        np.concatenate([table_high, table_high, table_low], axis=1),
        np.concatenate([gather_high, gather_high, gather_low], axis=1),
        np.ascontiguousarray(table.T),
    )


def kerr_kernel(
    x_ref, perm_ref, back_ref, spread_ref, table_ref, gather_ref, flip_ref, chi_ref, out_ref,
    xh, xl, p3, g1, r3, qh, ql,
):
    shards, _, local, _ = x_ref.shape
    groups = HG_ORDER // GROUP
    span = GROUP * HG_ORDER

    @pl.loop(0, shards)
    def _(s):
        value = jnp.concatenate([x_ref[s, c] for c in range(4)], axis=1)
        high, low = parts(value)
        rows = pl.ds(pl.multiple_of(s * local, local), local)
        xh[rows, :] = high
        xl[rows, :] = low

    @pl.loop(0, groups)
    def _(g):
        rows = pl.ds(pl.multiple_of(g * span, span), span)
        high = mm(perm_ref[rows, :], xh[...]).astype(bf16)
        p3[g, 0:span, :] = high
        p3[g, 2 * span : 3 * span, :] = high
        p3[g, span : 2 * span, :] = mm(perm_ref[rows, :], xl[...]).astype(bf16)

    points = 16
    for pair in range(groups // 2):

        @pl.loop(0, GRID // points)
        def _(b):
            rows = pl.ds(pl.multiple_of(b * points * GROUP, points * GROUP), points * GROUP)
            ys = pl.ds(b * points, points)
            both = [
                mm(spread_ref[rows, :], p3[2 * pair + i]).reshape(points, GROUP, 4 * LANES)
                for i in range(2)
            ]
            high, low = parts(jnp.concatenate(both, axis=1))
            g1[ys, pair * 16 : pair * 16 + 16, :] = high
            g1[ys, HG_ORDER + pair * 16 : HG_ORDER + pair * 16 + 16, :] = low

    def line(y):
        stored = g1[y]
        grid = mm(table_ref[...], jnp.concatenate([stored, stored[:HG_ORDER]], axis=0))
        er, ei, cr, ci = (grid[:, i * LANES : (i + 1) * LANES] for i in range(4))
        rr, ii = er * er, ei * ei
        intensity = rr + ii
        cross = 2.0 * er * ei
        real = (intensity + 2.0 * rr) * ci - cross * cr
        imag = cross * ci - (intensity + 2.0 * ii) * cr
        high, low = parts(jnp.concatenate([real, imag], axis=1))
        weight_high, weight_low = parts(flip_ref[...] * chi_ref[pl.ds(y, 1), :])
        weights = jnp.concatenate([weight_high, weight_high, weight_low], axis=1)
        return mm(weights, jnp.concatenate([high, low, high], axis=0))

    total = GRID * GROUP
    step_lines = 4

    @pl.loop(0, GRID // step_lines)
    def _(b):
        got = [line(b * step_lines + i) for i in range(step_lines)]
        rows = step_lines * GROUP
        at = pl.multiple_of(b * rows, rows)
        for g in range(groups):
            high, low = parts(
                jnp.concatenate([v[g * GROUP : (g + 1) * GROUP] for v in got], axis=0)
            )
            r3[g, pl.ds(at, rows), :] = high
            r3[g, pl.ds(total + at, rows), :] = low
            r3[g, pl.ds(2 * total + at, rows), :] = high

    @pl.loop(0, groups)
    def _(g):
        high, low = parts(mm(gather_ref[...], r3[g]))
        rows = pl.ds(pl.multiple_of(g * span, span), span)
        qh[rows, :] = high
        ql[rows, :] = low

    @pl.loop(0, shards)
    def _(s):
        rows = pl.ds(pl.multiple_of(s * local, local), local)
        value = mm(back_ref[rows, :], qh[...]) + mm(back_ref[rows, :], ql[...])
        out_ref[s, 0] = value[:, :LANES]
        out_ref[s, 1] = value[:, LANES:]


def kerr_call(received, perm, back, chi_lines):
    shards, _, local, _ = received.shape
    modes = shards * local
    groups = HG_ORDER // GROUP
    spread, table, gather, flip = kerr_constants()
    operands = (received, perm, back, spread, table, gather, flip, chi_lines)
    return pl.pallas_call(
        kerr_kernel,
        out_shape=jax.ShapeDtypeStruct((shards, 2, local, LANES), f32),
        in_specs=[pl.BlockSpec(memory_space=pltpu.VMEM)] * len(operands),
        out_specs=pl.BlockSpec(memory_space=pltpu.VMEM),
        scratch_shapes=[
            pltpu.VMEM((modes, 4 * LANES), bf16),
            pltpu.VMEM((modes, 4 * LANES), bf16),
            pltpu.VMEM((groups, 3 * GROUP * HG_ORDER, 4 * LANES), bf16),
            pltpu.VMEM((GRID, 2 * HG_ORDER, 4 * LANES), bf16),
            pltpu.VMEM((groups, 3 * GRID * GROUP, 2 * LANES), bf16),
            pltpu.VMEM((modes, 2 * LANES), bf16),
            pltpu.VMEM((modes, 2 * LANES), bf16),
        ],
        compiler_params=pltpu.CompilerParams(vmem_limit_bytes=48 << 20),
        cost_estimate=pl.CostEstimate(
            flops=30_000_000_000, bytes_accessed=12 << 20, transcendentals=0
        ),
        name="kerr_chunk",
    )(*operands)


def small_fft(values, sign):
    count = len(values)
    if count == 1:
        return values
    evens = small_fft(values[0::2], sign)
    odds = small_fft(values[1::2], sign)
    lower, upper = [], []
    for k in range(count // 2):
        er, ei = evens[k]
        dr, di = odds[k]
        if k == 0:
            tr, ti = dr, di
        elif 4 * k == count:
            tr, ti = (-di, dr) if sign > 0 else (di, -dr)
        else:
            c = math.cos(2 * math.pi * k / count)
            s = sign * math.sin(2 * math.pi * k / count)
            tr, ti = dr * c - di * s, dr * s + di * c
        lower.append((er + tr, ei + ti))
        upper.append((er - tr, ei - ti))
    return lower + upper


def dispersion_constants(length):
    outer = length // LANES
    k = np.arange(outer)[:, None] * np.arange(LANES)[None, :] % length
    twiddle = np.stack([np.cos(2 * np.pi * k / length), np.sin(2 * np.pi * k / length)])
    angle = 2 * np.pi * (np.arange(LANES)[:, None] * np.arange(LANES)[None, :] % LANES) / LANES
    c, s = np.cos(angle), np.sin(angle)
    out = [twiddle.astype(np.float32)]
    for sign in (-1.0, 1.0):
        high, low = host_parts(np.block([[c, sign * s], [-sign * s, c]]))
        out.append(np.concatenate([high, high, low], axis=0))
    return out


def dispersion_kernel(chunks, *refs):
    sources = refs[:chunks]
    cos_ref, sin_ref, tw_ref, fore_ref, back_ref, out_ref, work = refs[chunks:]
    shards = sources[0].shape[0]
    outer, rows, _ = cos_ref.shape
    scale = 1.0 / (outer * LANES)

    def triple(value):
        high, low = parts(value)
        return jnp.concatenate([high, low, high], axis=1)

    for h in range(rows // 8):
        at = slice(h * 8, h * 8 + 8)
        signal = [
            (sources[a // shards][a % shards, 0, at, :], sources[a // shards][a % shards, 1, at, :])
            for a in range(outer)
        ]
        for k, (re, im) in enumerate(small_fft(signal, -1)):
            c, s = tw_ref[0, k : k + 1, :], tw_ref[1, k : k + 1, :]
            work[k, at, 0:LANES] = re * c + im * s
            work[k, at, LANES : 2 * LANES] = im * c - re * s

    block = 8
    for b in range(outer // block):
        ks = slice(b * block, (b + 1) * block)
        value = work[ks].reshape(block * rows, 2 * LANES)
        value = mm(triple(value), fore_ref[...])
        re, im = value[:, :LANES], value[:, LANES:]
        c = cos_ref[ks].reshape(block * rows, LANES)
        s = sin_ref[ks].reshape(block * rows, LANES)
        value = jnp.concatenate([re * c + im * s, im * c - re * s], axis=1)
        value = mm(triple(value), back_ref[...])
        work[ks] = value.reshape(block, rows, 2 * LANES)

    for h in range(rows // 8):
        at = slice(h * 8, h * 8 + 8)
        spectrum = []
        for k in range(outer):
            re, im = work[k, at, 0:LANES], work[k, at, LANES : 2 * LANES]
            c, s = tw_ref[0, k : k + 1, :] * scale, tw_ref[1, k : k + 1, :] * scale
            spectrum.append((re * c - im * s, re * s + im * c))
        for a, (re, im) in enumerate(small_fft(spectrum, 1)):
            out_ref[0, 0, at, a * LANES : (a + 1) * LANES] = re
            out_ref[0, 1, at, a * LANES : (a + 1) * LANES] = im


def dispersion_call(sources, cos, sin):
    shards, _, modes, _ = sources[0].shape
    outer = cos.shape[0]
    length = outer * LANES
    rows = 16
    twiddle, fore, back = dispersion_constants(length)
    whole = lambda a: pl.BlockSpec(a.shape, lambda i: (0,) * a.ndim)
    return pl.pallas_call(
        functools.partial(dispersion_kernel, len(sources)),
        grid=(modes // rows,),
        out_shape=jax.ShapeDtypeStruct((1, 2, modes, length), f32),
        in_specs=[pl.BlockSpec((shards, 2, rows, LANES), lambda i: (0, 0, i, 0))] * len(sources)
        + [pl.BlockSpec((outer, rows, LANES), lambda i: (0, i, 0))] * 2
        + [whole(twiddle), whole(fore), whole(back)],
        out_specs=pl.BlockSpec((1, 2, rows, length), lambda i: (0, 0, i, 0)),
        scratch_shapes=[pltpu.VMEM((outer, rows, 2 * LANES), f32)],
        compiler_params=pltpu.CompilerParams(vmem_limit_bytes=40 << 20),
        cost_estimate=pl.CostEstimate(
            flops=4_000_000_000, bytes_accessed=16 << 20, transcendentals=0
        ),
        name="dispersion",
    )(*sources, cos, sin, twiddle, fore, back)


def on_device(forward, cotangent, mode_order, region, chi, phase, loss):
    shards = lax.axis_size("ma")
    depth = lax.axis_size("gz")
    local, length = forward.shape[2], forward.shape[3]
    modes = mode_order.shape[0]
    width = shards * LANES
    chunks = length // width
    outer = length // LANES

    order = jnp.arange(modes, dtype=jnp.int32)
    perm = (order[:, None] == mode_order[None, :]).astype(bf16)
    back = (mode_order[:, None] == order[None, :]).astype(bf16)
    matches = region.T[:, :, None] == jnp.arange(REGIONS, dtype=jnp.int32)[None, None, :]
    chi_lines = gamma_kerr * jnp.sum(jnp.where(matches, chi[None, None, :], 0.0), axis=-1)

    def chunk(array, c):
        piece = array[0, :, :, c * width : (c + 1) * width]
        return piece.reshape(2, local, shards, LANES).transpose(2, 0, 1, 3)

    cots = [chunk(cotangent, c) for c in range(chunks)]
    received = [
        lax.all_to_all(
            jnp.concatenate([chunk(forward, c), cots[c]], axis=1), "ma", 0, 0, tiled=True
        )
        for c in range(chunks)
    ]
    turned = phase.reshape(local, LANES, outer).transpose(2, 0, 1)
    cos, sin = jnp.cos(turned), jnp.sin(turned)

    to_even = [(i + 1, i) for i in range(0, depth, 2)]
    to_odd = [(i, i + 1) for i in range(0, depth, 2)]
    to_chip = [(i + 2, i) for i in range(0, depth - 2, 2)]
    own = loss[0][None, None, :, None]
    pair = (loss[0] * lax.ppermute(loss[0], "gz", to_even))[None, None, :, None]

    sources = []
    for c in range(chunks):
        kerr = kerr_call(received[c], perm, back, chi_lines)
        source = cots[c] + lax.all_to_all(kerr, "ma", 0, 0, tiled=True)
        both = source + own * lax.ppermute(source, "gz", to_even)
        value, later = both, jnp.zeros_like(both)
        for _ in range(depth // 2 - 1):
            later = lax.ppermute(value, "gz", to_chip)
            value = both + pair * later
        sources.append(value + own * lax.ppermute(later, "gz", to_odd))
    return dispersion_call(sources, cos, sin)


def solution(mesh):
    in_specs = (
        P("gz", None, "ma", None),
        P("gz", None, "ma", None),
        P(),
        P(),
        P(),
        P("ma", None),
        P("gz", "ma"),
    )
    out_specs = P("gz", None, "ma", None)
    return jax.shard_map(
        on_device, mesh=mesh, in_specs=in_specs, out_specs=out_specs, check_vma=False
    )
```

time: 877 us -> 514 us (0.59)
  matrix products: 253 us -> 0 us
  Pallas kernels: 0 us -> 204 us
  waiting for transfers between devices: 327 us -> 186 us
  other arithmetic: 128 us -> 25.6 us
  local copies, waits for them, and re-layouts: 129 us -> 30.8 us
  starting transfers between devices: 16.5 us -> 65.7 us
  between operations: 14 us -> 0.63 us
    dot_general x22 -> x0, matrix products: 253 us -> none  [the longest x2 118 us: modes_to_grid(): jnp.einsum('...pyt,xp->...xyt', partial_grid, table, precision=lax.Precis...]
    pallas_call x0 -> x5, Pallas kernels: none -> 204 us  [the longest x4 194 us: kerr_call(): pl.pallas_call(kerr_kernel, out_shape=jax.ShapeDtypeStruct((shards, 2, lo...]
    all_gather x1 -> x0, waiting for transfers between devices: 94.7 us -> none  [prefix(): everything = jax.tree.map(lambda part: lax.all_gather(part, axis), shard)]
    all_to_all x3 -> x8, waiting for transfers between devices: 233 us -> 148 us  [the longest x4 134 us: on_device(): lax.all_to_all(jnp.concatenate([chunk(forward, c), cots[c]], axis=1), 'ma...]
    mul x4 -> x2, other arithmetic: 68.8 us -> 0.01 us  [the longest x1 0.01 us: on_device(): gamma_kerr * jnp.sum(jnp.where(matches, chi[None, None, :], 0.0), axis=-1)]
    gather x3 -> x0, local copies, waits for them, and re-layouts: 41.4 us -> none  [the longest x2 27.6 us: ordered_grid(): ordered = jnp.take(fields, inverse, axis=-2)]
    ppermute x0 -> x13, waiting for transfers between devices: none -> 38.4 us  [the longest x4 35.2 us: on_device(): later = lax.ppermute(value, 'gz', to_chip)]
    select_n x5 -> x0, other arithmetic: 32.6 us -> none  [the longest x4 25.3 us: turn(): return jax.tree.map(lambda a, b: jnp.where(reached, a, b), new, before)]
  transfers between devices with their start and end apart: 4 -> 21, of which waited for: 4 -> 9; matrix products, arithmetic and copies ran while one was open for 6% -> 6% of each run, Pallas kernels for 0% -> 38%
where the time goes in v1:
time: 514 us; the launch traced here: 512 us
  Pallas kernels  204 us (40%)
  waiting for transfers between devices  186 us (36%)
  starting transfers between devices  65.7 us (13%)
  local copies, waits for them, and re-layouts  30.8 us (6%)
  other arithmetic  25.6 us (5%)
    pallas_call x4, Pallas kernels, kerr_call(): pl.pallas_call(kerr_kernel, out_shape=jax.ShapeDtypeStruct((shards, 2, lo...  194 us
    all_to_all x4, waiting for transfers between devices, on_device(): lax.all_to_all(jnp.concatenate([chunk(forward, c), cots[c]], axis=1), 'ma...  134 us
    ppermute x4, waiting for transfers between devices, on_device(): later = lax.ppermute(value, 'gz', to_chip)  35.2 us
    all_to_all x4, starting transfers between devices, on_device(): source = cots[c] + lax.all_to_all(kerr, 'ma', 0, 0, tiled=True)  24 us
    all_to_all x4, starting transfers between devices, on_device(): lax.all_to_all(jnp.concatenate([chunk(forward, c), cots[c]], axis=1), 'ma...  20.5 us
    all_to_all x4, waiting for transfers between devices, on_device(): source = cots[c] + lax.all_to_all(kerr, 'ma', 0, 0, tiled=True)  14 us
    sin x2, local copies, waits for them, and re-layouts, on_device(): cos, sin = (jnp.cos(turned), jnp.sin(turned))  11.1 us
  transfers between devices with their start and end apart: 21, of which 9 were waited for; matrix products, arithmetic and copies ran while one was open for 6% of the time, Pallas kernels for 38%

profile of v1, /device:TPU:0, one launch (start us, length us, event | category | flops | bytes accessed | tf_op | source)
XLA Modules:
  0.0 512.5 jit_solution(8130732967390909274)
XLA Ops:
  4.6 4.4 fusion.2
  11.2 7.4 %all-to-all-start = ((f32[8,4,128,128]{3,2,1,0:T(8,128)}), f32[8,4,128,128]{3,2,1,0:T(8,128)}, u32[]{:S(2)}, u32[]{:S(2)}) async-start(f32[8,4,128,128]{3,2,1,0:T(8,128)} %pad_maximum_fusion), calls=%async_computation | async-start | bytes 4194304 | tf_op jit(solution)/shard_map/all_to_all | solution.py:311
  22.0 45.0 %all-to-all-done.x_ref = f32[8,4,128,128]{3,2,1,0:T(8,128)} async-done(((f32[8,4,128,128]{3,2,1,0:T(8,128)}), f32[8,4,128,128]{3,2,1,0:T(8,128)}, u32[]{:S(2)}, u32[]{:S(2)}) %all-to-all-start) | async-done | bytes 2097184 | tf_op jit(solution)/shard_map/all_to_all | solution.py:311
  67.0 4.4 all-to-all-start.4
  74.8 44.4 %all-to-all-done.4.x_ref = f32[8,4,128,128]{3,2,1,0:T(8,128)} async-done(((f32[8,4,128,128]{3,2,1,0:T(8,128)}), f32[8,4,128,128]{3,2,1,0:T(8,128)}, u32[]{:S(2)}, u32[]{:S(2)}) %all-to-all-start.4) | async-done | bytes 2097184 | tf_op jit(solution)/shard_map/all_to_all | solution.py:311
  119.1 4.4 all-to-all-start.2
  126.9 44.4 %all-to-all-done.2.x_ref = f32[8,4,128,128]{3,2,1,0:T(8,128)} async-done(((f32[8,4,128,128]{3,2,1,0:T(8,128)}), f32[8,4,128,128]{3,2,1,0:T(8,128)}, u32[]{:S(2)}, u32[]{:S(2)}) %all-to-all-start.2) | async-done | bytes 2097184 | tf_op jit(solution)/shard_map/all_to_all | solution.py:311
  171.3 4.4 all-to-all-start.6
  179.2 48.5 %kerr_chunk.4 = f32[8,2,128,128]{3,2,1,0:T(8,128)} custom-call(f32[8,4,128,128]{3,2,1,0:T(8,128)} %all-to-all-done.x_ref, bf16[1024,1024]{1,0:T(8,128)(2,1)} %get-tuple-element.16.perm_ref, bf16[1024,1024]{1,0:T(8,128)(2,1)} %get-tuple-element.15.back_ref, bf16[1024,768]{1,0:T(8,128)(2,1)S(1)} %copy-done.1, bf16[128,96]{1,0:T(8,128)(2,1)S(1)} %copy-done.6, ...), custom_call_target="tpu_custom_call" | custom-call | flops 30000001024 | bytes 12582912 | tf_op jit(solution)/shard_map/kerr_chunk/pallas_call | solution.py:162
  227.7 5.9 %all-to-all-start.1 = ((f32[8,2,128,128]{3,2,1,0:T(8,128)}), f32[8,2,128,128]{3,2,1,0:T(8,128)}, u32[]{:S(2)}, u32[]{:S(2)}) async-start(f32[8,2,128,128]{3,2,1,0:T(8,128)} %kerr_chunk.4), calls=%async_computation.1 | async-start | bytes 2097152 | tf_op jit(solution)/shard_map/all_to_all | solution.py:328
  233.6 48.5 %kerr_chunk.6 = f32[8,2,128,128]{3,2,1,0:T(8,128)} custom-call(f32[8,4,128,128]{3,2,1,0:T(8,128)} %all-to-all-done.4.x_ref, bf16[1024,1024]{1,0:T(8,128)(2,1)} %get-tuple-element.16.perm_ref, bf16[1024,1024]{1,0:T(8,128)(2,1)} %get-tuple-element.15.back_ref, bf16[1024,768]{1,0:T(8,128)(2,1)S(1)} %copy-done.1, bf16[128,96]{1,0:T(8,128)(2,1)S(1)} %copy-done.6, ...), custom_call_target="tpu_custom_call" | custom-call | flops 30000001024 | bytes 12582912 | tf_op jit(solution)/shard_map/kerr_chunk/pallas_call | solution.py:162
  282.1 6.0 %all-to-all-start.5 = ((f32[8,2,128,128]{3,2,1,0:T(8,128)}), f32[8,2,128,128]{3,2,1,0:T(8,128)}, u32[]{:S(2)}, u32[]{:S(2)}) async-start(f32[8,2,128,128]{3,2,1,0:T(8,128)} %kerr_chunk.6), calls=%async_computation.5 | async-start | bytes 2097152 | tf_op jit(solution)/shard_map/all_to_all | solution.py:328
  288.1 48.5 %kerr_chunk.5 = f32[8,2,128,128]{3,2,1,0:T(8,128)} custom-call(f32[8,4,128,128]{3,2,1,0:T(8,128)} %all-to-all-done.2.x_ref, bf16[1024,1024]{1,0:T(8,128)(2,1)} %get-tuple-element.16.perm_ref, bf16[1024,1024]{1,0:T(8,128)(2,1)} %get-tuple-element.15.back_ref, bf16[1024,768]{1,0:T(8,128)(2,1)S(1)} %copy-done.1, bf16[128,96]{1,0:T(8,128)(2,1)S(1)} %copy-done.6, ...), custom_call_target="tpu_custom_call" | custom-call | flops 30000001024 | bytes 12582912 | tf_op jit(solution)/shard_map/kerr_chunk/pallas_call | solution.py:162
  336.6 6.0 %all-to-all-start.3 = ((f32[8,2,128,128]{3,2,1,0:T(8,128)}), f32[8,2,128,128]{3,2,1,0:T(8,128)}, u32[]{:S(2)}, u32[]{:S(2)}) async-start(f32[8,2,128,128]{3,2,1,0:T(8,128)} %kerr_chunk.5), calls=%async_computation.3 | async-start | bytes 2097152 | tf_op jit(solution)/shard_map/all_to_all | solution.py:328
  342.6 48.5 %kerr_chunk.7 = f32[8,2,128,128]{3,2,1,0:T(8,128)} custom-call(f32[8,4,128,128]{3,2,1,0:T(8,128)} %all-to-all-done.6.x_ref, bf16[1024,1024]{1,0:T(8,128)(2,1)} %get-tuple-element.16.perm_ref, bf16[1024,1024]{1,0:T(8,128)(2,1)} %get-tuple-element.15.back_ref, bf16[1024,768]{1,0:T(8,128)(2,1)S(1)} %copy-done.1, bf16[128,96]{1,0:T(8,128)(2,1)S(1)} %copy-done.6, ...), custom_call_target="tpu_custom_call" | custom-call | flops 30000001024 | bytes 12582912 | tf_op jit(solution)/shard_map/kerr_chunk/pallas_call | solution.py:162
  391.1 6.1 %all-to-all-start.7 = ((f32[8,2,128,128]{3,2,1,0:T(8,128)}), f32[8,2,128,128]{3,2,1,0:T(8,128)}, u32[]{:S(2)}, u32[]{:S(2)}) async-start(f32[8,2,128,128]{3,2,1,0:T(8,128)} %kerr_chunk.7), calls=%async_computation.7 | async-start | bytes 2097152 | tf_op jit(solution)/shard_map/all_to_all | solution.py:328
  406.6 14.0 %all-to-all-done.7 = f32[8,2,128,128]{3,2,1,0:T(8,128)} async-done(((f32[8,2,128,128]{3,2,1,0:T(8,128)}), f32[8,2,128,128]{3,2,1,0:T(8,128)}, u32[]{:S(2)}, u32[]{:S(2)}) %all-to-all-start.7) | async-done | bytes 1048608 | tf_op jit(solution)/shard_map/all_to_all | solution.py:328
  439.2 8.4 %collective-permute-done.11 = f32[8,2,128,128]{3,2,1,0:T(8,128)} collective-permute-done((f32[8,2,128,128]{3,2,1,0:T(8,128)S(1)}, f32[8,2,128,128]{3,2,1,0:T(8,128)}, u32[]{:S(2)}, u32[]{:S(2)}) %collective-permute-start.11) | collective-permute-done | bytes 1048608 | tf_op jit(solution)/shard_map/ppermute | solution.py:332
  449.8 9.0 %collective-permute-done.2 = f32[8,2,128,128]{3,2,1,0:T(8,128)} collective-permute-done((f32[8,2,128,128]{3,2,1,0:T(8,128)}, f32[8,2,128,128]{3,2,1,0:T(8,128)}, u32[]{:S(2)}, u32[]{:S(2)}) %collective-permute-start.2) | collective-permute-done | bytes 1048608 | tf_op jit(solution)/shard_map/ppermute | solution.py:332
  461.1 8.9 %collective-permute-done.5 = f32[8,2,128,128]{3,2,1,0:T(8,128)} collective-permute-done((f32[8,2,128,128]{3,2,1,0:T(8,128)}, f32[8,2,128,128]{3,2,1,0:T(8,128)}, u32[]{:S(2)}, u32[]{:S(2)}) %collective-permute-start.5) | collective-permute-done | bytes 1048608 | tf_op jit(solution)/shard_map/ppermute | solution.py:332
  472.4 8.9 %collective-permute-done.8 = f32[8,2,128,128]{3,2,1,0:T(8,128)} collective-permute-done((f32[8,2,128,128]{3,2,1,0:T(8,128)}, f32[8,2,128,128]{3,2,1,0:T(8,128)}, u32[]{:S(2)}, u32[]{:S(2)}) %collective-permute-start.8) | collective-permute-done | bytes 1048608 | tf_op jit(solution)/shard_map/ppermute | solution.py:332
  483.5 8.2 %fusion.4 = (f32[128,4096]{0,1:T(8,128)}, f32[128,4096]{0,1:T(8,128)}) fusion(f32[128,4096]{0,1:T(8,128)S(1)} %copy.66), kind=kLoop, calls=%fused_computation.26 | loop fusion | bytes 6291456 | tf_op jit(solution)/shard_map/sin | solution.py:317
  496.8 5.9 %multiply_add_fusion = (f32[8,2,128,128]{3,2,1,0:T(8,128)S(1)}, f32[8,2,128,128]{3,2,1,0:T(8,128)S(1)}, f32[8,2,128,128]{3,2,1,0:T(8,128)S(1)}, f32[8,2,128,128]{3,2,1,0:T(8,128)S(1)}) fusion(f32[8,2,128,128]{3,2,1,0:T(8,128)} %collective-permute-done.12, f32[8,2,128,128]{3,2,1,0:T(8,128)S(1)} %get-tuple-element.21, ...), kind=kLoop, calls=%fused_computation.8 | loop fusion | flops 4194304 | bytes 16778240 | tf_op jit(solution)/shard_map/add | solution.py:334
  502.7 9.7 %dispersion.1 = f32[1,2,128,4096]{3,2,1,0:T(8,128)} custom-call(f32[8,2,128,128]{3,2,1,0:T(8,128)S(1)} %get-tuple-element.20.refs_0_, f32[8,2,128,128]{3,2,1,0:T(8,128)S(1)} %get-tuple-element.18.refs_1_, f32[8,2,128,128]{3,2,1,0:T(8,128)S(1)} %get-tuple-element.19.refs_2_, f32[8,2,128,128]{3,2,1,0:T(8,128)S(1)} %get-tuple-element.17.refs_3_, ...), custom_call_target="tpu_custom_call" | custom-call | flops 4000000000 | bytes 16777216 | tf_op jit(solution)/shard_map/dispersion/pallas_call | solution.py:273
  (112 shorter events, 62.3 us)
Async XLA Ops:
  11.2 55.8 %all-to-all-start = ((f32[8,4,128,128]{3,2,1,0:T(8,128)}), f32[8,4,128,128]{3,2,1,0:T(8,128)}, u32[]{:S(2)}, u32[]{:S(2)}) async-start(f32[8,4,128,128]{3,2,1,0:T(8,128)} %pad_maximum_fusion), calls=%async_computation | async-start | bytes 4194304 | tf_op jit(solution)/shard_map/all_to_all | solution.py:311
  22.0 49.3 %copy-start.18 = (f32[1,2,128,1024]{3,2,1,0:T(8,128)S(1)}, f32[1,2,128,1024]{3,2,1,0:T(8,128)}, u32[]{:S(2)}) copy-start(f32[1,2,128,1024]{3,2,1,0:T(8,128)} %get-tuple-element.11) | copy-start | bytes 3145732
  67.0 52.2 %all-to-all-start.4 = ((f32[8,4,128,128]{3,2,1,0:T(8,128)}), f32[8,4,128,128]{3,2,1,0:T(8,128)}, u32[]{:S(2)}, u32[]{:S(2)}) async-start(f32[8,4,128,128]{3,2,1,0:T(8,128)} %pad_maximum_fusion.2), calls=%async_computation.4 | async-start | bytes 4194304 | tf_op jit(solution)/shard_map/all_to_all | solution.py:311
  119.1 52.2 %all-to-all-start.2 = ((f32[8,4,128,128]{3,2,1,0:T(8,128)}), f32[8,4,128,128]{3,2,1,0:T(8,128)}, u32[]{:S(2)}, u32[]{:S(2)}) async-start(f32[8,4,128,128]{3,2,1,0:T(8,128)} %pad_maximum_fusion.1), calls=%async_computation.2 | async-start | bytes 4194304 | tf_op jit(solution)/shard_map/all_to_all | solution.py:311
  126.9 48.9 %copy-start.25 = (f32[8]{0:T(128)S(1)}, f32[8]{0:T(128)}, u32[]{:S(2)}) copy-start(f32[8]{0:T(128)} %param.30) | copy-start | bytes 100
  126.9 49.2 %copy-start.23 = (s32[1024]{0:T(1024)S(1)}, s32[1024]{0:T(1024)}, u32[]{:S(2)}) copy-start(s32[1024]{0:T(1024)} %param.28) | copy-start | bytes 12292
  171.3 56.4 %all-to-all-start.6 = ((f32[8,4,128,128]{3,2,1,0:T(8,128)}), f32[8,4,128,128]{3,2,1,0:T(8,128)}, u32[]{:S(2)}, u32[]{:S(2)}) async-start(f32[8,4,128,128]{3,2,1,0:T(8,128)} %pad_maximum_fusion.3), calls=%async_computation.6 | async-start | bytes 4194304 | tf_op jit(solution)/shard_map/all_to_all | solution.py:311
  227.7 54.3 %all-to-all-start.1 = ((f32[8,2,128,128]{3,2,1,0:T(8,128)}), f32[8,2,128,128]{3,2,1,0:T(8,128)}, u32[]{:S(2)}, u32[]{:S(2)}) async-start(f32[8,2,128,128]{3,2,1,0:T(8,128)} %kerr_chunk.4), calls=%async_computation.1 | async-start | bytes 2097152 | tf_op jit(solution)/shard_map/all_to_all | solution.py:328
  282.1 54.5 %all-to-all-start.5 = ((f32[8,2,128,128]{3,2,1,0:T(8,128)}), f32[8,2,128,128]{3,2,1,0:T(8,128)}, u32[]{:S(2)}, u32[]{:S(2)}) async-start(f32[8,2,128,128]{3,2,1,0:T(8,128)} %kerr_chunk.6), calls=%async_computation.5 | async-start | bytes 2097152 | tf_op jit(solution)/shard_map/all_to_all | solution.py:328
  336.6 54.5 %all-to-all-start.3 = ((f32[8,2,128,128]{3,2,1,0:T(8,128)}), f32[8,2,128,128]{3,2,1,0:T(8,128)}, u32[]{:S(2)}, u32[]{:S(2)}) async-start(f32[8,2,128,128]{3,2,1,0:T(8,128)} %kerr_chunk.5), calls=%async_computation.3 | async-start | bytes 2097152 | tf_op jit(solution)/shard_map/all_to_all | solution.py:328
  391.1 29.5 %all-to-all-start.7 = ((f32[8,2,128,128]{3,2,1,0:T(8,128)}), f32[8,2,128,128]{3,2,1,0:T(8,128)}, u32[]{:S(2)}, u32[]{:S(2)}) async-start(f32[8,2,128,128]{3,2,1,0:T(8,128)} %kerr_chunk.7), calls=%async_computation.7 | async-start | bytes 2097152 | tf_op jit(solution)/shard_map/all_to_all | solution.py:328
  398.6 24.6 %collective-permute-start = (f32[8,2,128,128]{3,2,1,0:T(8,128)S(1)}, f32[8,2,128,128]{3,2,1,0:T(8,128)}, u32[]{:S(2)}, u32[]{:S(2)}) collective-permute-start(f32[8,2,128,128]{3,2,1,0:T(8,128)S(1)} %bitcast_add_fusion.3), channel_id=1, source_target_pairs={{8,0},{24,16},{9,1},{25,17},{10,2},{26,18},{11,3},{27,19},{12,4},{... | collective-permute-start | bytes 3145736 | tf_op jit(solution)/shard_map/ppermute | solution.py:329
  401.4 21.8 %collective-permute-start.7 = (f32[8,2,128,128]{3,2,1,0:T(8,128)S(1)}, f32[8,2,128,128]{3,2,1,0:T(8,128)}, u32[]{:S(2)}, u32[]{:S(2)}) collective-permute-start(f32[8,2,128,128]{3,2,1,0:T(8,128)S(1)} %bitcast_add_fusion.1), channel_id=1, source_target_pairs={{8,0},{24,16},{9,1},{25,17},{10,2},{26,18},{11,3},{27,19},{12,4},{... | collective-permute-start | bytes 3145736 | tf_op jit(solution)/shard_map/ppermute | solution.py:329
  405.2 18.1 %collective-permute-start.4 = (f32[8,2,128,128]{3,2,1,0:T(8,128)}, f32[8,2,128,128]{3,2,1,0:T(8,128)}, u32[]{:S(2)}, u32[]{:S(2)}) collective-permute-start(f32[8,2,128,128]{3,2,1,0:T(8,128)} %bitcast_add_fusion.2), channel_id=1, source_target_pairs={{8,0},{24,16},{9,1},{25,17},{10,2},{26,18},{11,3},{27,19},{12,4},{... | collective-permute-start | bytes 3145736 | tf_op jit(solution)/shard_map/ppermute | solution.py:329
  421.9 4.6 collective-permute-start.10
  430.8 16.8 %collective-permute-start.11 = (f32[8,2,128,128]{3,2,1,0:T(8,128)S(1)}, f32[8,2,128,128]{3,2,1,0:T(8,128)}, u32[]{:S(2)}, u32[]{:S(2)}) collective-permute-start(f32[8,2,128,128]{3,2,1,0:T(8,128)S(1)} %get-tuple-element.21), channel_id=1, source_target_pairs={{16,0},{17,1},{18,2},{19,3},{20,4},{21,5},{22,6},{23,7}} | collective-permute-start | bytes 3145736 | tf_op jit(solution)/shard_map/ppermute | solution.py:332
  432.1 26.7 %collective-permute-start.2 = (f32[8,2,128,128]{3,2,1,0:T(8,128)}, f32[8,2,128,128]{3,2,1,0:T(8,128)}, u32[]{:S(2)}, u32[]{:S(2)}) collective-permute-start(f32[8,2,128,128]{3,2,1,0:T(8,128)} %get-tuple-element.24), channel_id=1, source_target_pairs={{16,0},{17,1},{18,2},{19,3},{20,4},{21,5},{22,6},{23,7}} | collective-permute-start | bytes 3145736 | tf_op jit(solution)/shard_map/ppermute | solution.py:332
  433.4 36.7 %collective-permute-start.5 = (f32[8,2,128,128]{3,2,1,0:T(8,128)}, f32[8,2,128,128]{3,2,1,0:T(8,128)}, u32[]{:S(2)}, u32[]{:S(2)}) collective-permute-start(f32[8,2,128,128]{3,2,1,0:T(8,128)} %get-tuple-element.22), channel_id=1, source_target_pairs={{16,0},{17,1},{18,2},{19,3},{20,4},{21,5},{22,6},{23,7}} | collective-permute-start | bytes 3145736 | tf_op jit(solution)/shard_map/ppermute | solution.py:332
  434.7 46.6 %collective-permute-start.8 = (f32[8,2,128,128]{3,2,1,0:T(8,128)}, f32[8,2,128,128]{3,2,1,0:T(8,128)}, u32[]{:S(2)}, u32[]{:S(2)}) collective-permute-start(f32[8,2,128,128]{3,2,1,0:T(8,128)} %get-tuple-element.23), channel_id=1, source_target_pairs={{16,0},{17,1},{18,2},{19,3},{20,4},{21,5},{22,6},{23,7}} | collective-permute-start | bytes 3145736 | tf_op jit(solution)/shard_map/ppermute | solution.py:332
  436.0 60.7 %collective-permute-start.1 = (f32[128]{0:T(128)S(1)}, f32[128]{0:T(128)S(1)}, u32[]{:S(2)}, u32[]{:S(2)}) collective-permute-start(f32[128]{0:T(128)S(1)} %bitcast.49), channel_id=1, source_target_pairs={{8,0},{24,16},{9,1},{25,17},{10,2},{26,18},{11,3},{27,19},{12,4},{... | collective-permute-start | bytes 1544 | tf_op jit(solution)/shard_map/ppermute | solution.py:323
  447.6 49.2 %collective-permute-start.12 = (f32[8,2,128,128]{3,2,1,0:T(8,128)}, f32[8,2,128,128]{3,2,1,0:T(8,128)}, u32[]{:S(2)}, u32[]{:S(2)}) collective-permute-start(f32[8,2,128,128]{3,2,1,0:T(8,128)} %collective-permute-done.11), channel_id=1, source_target_pairs={{0,8},{16,24},{1,9},{17,25},{2,10},{18,26},{3,11},{19,27},{4,12},{... | collective-permute-start | bytes 3145736 | tf_op jit(solution)/shard_map/ppermute | solution.py:334
  458.8 37.9 %collective-permute-start.3 = (f32[8,2,128,128]{3,2,1,0:T(8,128)}, f32[8,2,128,128]{3,2,1,0:T(8,128)}, u32[]{:S(2)}, u32[]{:S(2)}) collective-permute-start(f32[8,2,128,128]{3,2,1,0:T(8,128)} %collective-permute-done.2), channel_id=1, source_target_pairs={{0,8},{16,24},{1,9},{17,25},{2,10},{18,26},{3,11},{19,27},{4,12},{... | collective-permute-start | bytes 3145736 | tf_op jit(solution)/shard_map/ppermute | solution.py:334
  470.0 26.7 %collective-permute-start.6 = (f32[8,2,128,128]{3,2,1,0:T(8,128)}, f32[8,2,128,128]{3,2,1,0:T(8,128)}, u32[]{:S(2)}, u32[]{:S(2)}) collective-permute-start(f32[8,2,128,128]{3,2,1,0:T(8,128)} %collective-permute-done.5), channel_id=1, source_target_pairs={{0,8},{16,24},{1,9},{17,25},{2,10},{18,26},{3,11},{19,27},{4,12},{... | collective-permute-start | bytes 3145736 | tf_op jit(solution)/shard_map/ppermute | solution.py:334
  481.3 15.5 %collective-permute-start.9 = (f32[8,2,128,128]{3,2,1,0:T(8,128)}, f32[8,2,128,128]{3,2,1,0:T(8,128)}, u32[]{:S(2)}, u32[]{:S(2)}) collective-permute-start(f32[8,2,128,128]{3,2,1,0:T(8,128)} %collective-permute-done.8), channel_id=1, source_target_pairs={{0,8},{16,24},{1,9},{17,25},{2,10},{18,26},{3,11},{19,27},{4,12},{... | collective-permute-start | bytes 3145736 | tf_op jit(solution)/shard_map/ppermute | solution.py:334
  (23 other events, 207.1 us)

commit v2 on v1

--- a/solution.py
+++ b/solution.py
@@ -70,9 +70,9 @@
 
 
 def kerr_kernel(
-    x_ref, perm_ref, back_ref, spread_ref, table_ref, gather_ref, flip_ref, chi_ref, out_ref,
-    xh, xl, p3, g1, r3, qh, ql,
+    x_ref, perm_ref, back_ref, spread_ref, table_ref, gather_ref, flip_ref, chi_ref, *refs
 ):
+    out_ref, xh, xl, p3, g1, r3, qh, ql = refs[-8:]
     shards, _, local, _ = x_ref.shape
     groups = HG_ORDER // GROUP
     span = GROUP * HG_ORDER
@@ -149,11 +149,11 @@
     def _(s):
         rows = pl.ds(pl.multiple_of(s * local, local), local)
         value = mm(back_ref[rows, :], qh[...]) + mm(back_ref[rows, :], ql[...])
-        out_ref[s, 0] = value[:, :LANES]
-        out_ref[s, 1] = value[:, LANES:]
-
-
-def kerr_call(received, perm, back, chi_lines):
+        out_ref[s, 0] = x_ref[s, 2] + value[:, :LANES]
+        out_ref[s, 1] = x_ref[s, 3] + value[:, LANES:]
+
+
+def kerr_call(received, perm, back, chi_lines, before=()):
     shards, _, local, _ = received.shape
     modes = shards * local
     groups = HG_ORDER // GROUP
@@ -162,7 +162,8 @@
     return pl.pallas_call(
         kerr_kernel,
         out_shape=jax.ShapeDtypeStruct((shards, 2, local, LANES), f32),
-        in_specs=[pl.BlockSpec(memory_space=pltpu.VMEM)] * len(operands),
+        in_specs=[pl.BlockSpec(memory_space=pltpu.VMEM)] * len(operands)
+        + [pl.BlockSpec(memory_space=pl.ANY)] * len(before),
         out_specs=pl.BlockSpec(memory_space=pltpu.VMEM),
         scratch_shapes=[
             pltpu.VMEM((modes, 4 * LANES), bf16),
@@ -178,7 +179,54 @@
             flops=30_000_000_000, bytes_accessed=12 << 20, transcendentals=0
         ),
         name="kerr_chunk",
-    )(*operands)
+    )(*operands, *before)
+
+
+def pack_kernel(forward_ref, cot_ref, *refs):
+    out_ref = refs[-1]
+    out_ref[0, 0:2] = forward_ref[0]
+    out_ref[0, 2:4] = cot_ref[0]
+
+
+def pack_call(forward, cotangent, c, shards, before=()):
+    local = forward.shape[2]
+    piece = pl.BlockSpec((1, 2, local, LANES), lambda i: (0, 0, 0, c * shards + i))
+    return pl.pallas_call(
+        pack_kernel,
+        grid=(shards,),
+        out_shape=jax.ShapeDtypeStruct((shards, 4, local, LANES), f32),
+        in_specs=[piece, piece] + [pl.BlockSpec(memory_space=pl.ANY)] * len(before),
+        out_specs=pl.BlockSpec((1, 4, local, LANES), lambda i: (i, 0, 0, 0)),
+        compiler_params=pltpu.CompilerParams(vmem_limit_bytes=16 << 20),
+        cost_estimate=pl.CostEstimate(flops=0, bytes_accessed=4 << 20, transcendentals=0),
+        name="pack_chunk",
+    )(forward, cotangent, *before)
+
+
+def carry_kernel(factor_ref, *refs):
+    out_ref = refs[-1]
+    for i in range(len(refs) // 2):
+        for c in range(2):
+            value, later = refs[2 * i][0, c], refs[2 * i + 1][0, c]
+            out_ref[0, 2 * i + c] = value + factor_ref[0] * later
+
+
+def carry_call(pairs, factor):
+    shards, _, local, _ = pairs[0][0].shape
+    piece = pl.BlockSpec((1, 2, local, LANES), lambda i: (i, 0, 0, 0))
+    flat = [array for pair in pairs for array in pair]
+    return pl.pallas_call(
+        carry_kernel,
+        grid=(shards,),
+        out_shape=jax.ShapeDtypeStruct((shards, len(flat), local, LANES), f32),
+        in_specs=[pl.BlockSpec((1, local, LANES), lambda i: (i, 0, 0))] + [piece] * len(flat),
+        out_specs=pl.BlockSpec((1, len(flat), local, LANES), lambda i: (i, 0, 0, 0)),
+        compiler_params=pltpu.CompilerParams(vmem_limit_bytes=16 << 20),
+        cost_estimate=pl.CostEstimate(
+            flops=0, bytes_accessed=(len(pairs) * 3) << 20, transcendentals=0
+        ),
+        name="carry",
+    )(factor, *flat)
 
 
 def small_fft(values, sign):
@@ -231,8 +279,10 @@
     for h in range(rows // 8):
         at = slice(h * 8, h * 8 + 8)
         signal = [
-            (sources[a // shards][a % shards, 0, at, :], sources[a // shards][a % shards, 1, at, :])
-            for a in range(outer)
+            (ref[d, 2 * c, at, :], ref[d, 2 * c + 1, at, :])
+            for ref in sources
+            for c in range(ref.shape[1] // 2)
+            for d in range(shards)
         ]
         for k, (re, im) in enumerate(small_fft(signal, -1)):
             c, s = tw_ref[0, k : k + 1, :], tw_ref[1, k : k + 1, :]
@@ -264,7 +314,7 @@
 
 
 def dispersion_call(sources, cos, sin):
-    shards, _, modes, _ = sources[0].shape
+    modes = sources[0].shape[2]
     outer = cos.shape[0]
     length = outer * LANES
     rows = 16
@@ -274,7 +324,9 @@
         functools.partial(dispersion_kernel, len(sources)),
         grid=(modes // rows,),
         out_shape=jax.ShapeDtypeStruct((1, 2, modes, length), f32),
-        in_specs=[pl.BlockSpec((shards, 2, rows, LANES), lambda i: (0, 0, i, 0))] * len(sources)
+        in_specs=[
+            pl.BlockSpec(a.shape[:2] + (rows, LANES), lambda i: (0, 0, i, 0)) for a in sources
+        ]
         + [pl.BlockSpec((outer, rows, LANES), lambda i: (0, i, 0))] * 2
         + [whole(twiddle), whole(fore), whole(back)],
         out_specs=pl.BlockSpec((1, 2, rows, length), lambda i: (0, 0, i, 0)),
@@ -302,37 +354,44 @@
     matches = region.T[:, :, None] == jnp.arange(REGIONS, dtype=jnp.int32)[None, None, :]
     chi_lines = gamma_kerr * jnp.sum(jnp.where(matches, chi[None, None, :], 0.0), axis=-1)
 
-    def chunk(array, c):
-        piece = array[0, :, :, c * width : (c + 1) * width]
-        return piece.reshape(2, local, shards, LANES).transpose(2, 0, 1, 3)
-
-    cots = [chunk(cotangent, c) for c in range(chunks)]
-    received = [
-        lax.all_to_all(
-            jnp.concatenate([chunk(forward, c), cots[c]], axis=1), "ma", 0, 0, tiled=True
-        )
-        for c in range(chunks)
-    ]
     turned = phase.reshape(local, LANES, outer).transpose(2, 0, 1)
     cos, sin = jnp.cos(turned), jnp.sin(turned)
 
     to_even = [(i + 1, i) for i in range(0, depth, 2)]
     to_odd = [(i, i + 1) for i in range(0, depth, 2)]
     to_chip = [(i + 2, i) for i in range(0, depth - 2, 2)]
-    own = loss[0][None, None, :, None]
-    pair = (loss[0] * lax.ppermute(loss[0], "gz", to_even))[None, None, :, None]
-
-    sources = []
-    for c in range(chunks):
-        kerr = kerr_call(received[c], perm, back, chi_lines)
-        source = cots[c] + lax.all_to_all(kerr, "ma", 0, 0, tiled=True)
-        both = source + own * lax.ppermute(source, "gz", to_even)
+    kept = lax.all_gather(loss[0], "ma")
+    wide = (shards, local, LANES)
+    own = jnp.broadcast_to(kept[:, :, None], wide)
+    pair = jnp.broadcast_to((kept * lax.ppermute(kept, "gz", to_even))[:, :, None], wide)
+
+    def exchange(array):
+        return lax.all_to_all(array, "ma", 0, 0, tiled=True)
+
+    def scan(source):
+        both = carry_call([(source, lax.ppermute(source, "gz", to_even))], own)
         value, later = both, jnp.zeros_like(both)
         for _ in range(depth // 2 - 1):
             later = lax.ppermute(value, "gz", to_chip)
-            value = both + pair * later
-        sources.append(value + own * lax.ppermute(later, "gz", to_odd))
-    return dispersion_call(sources, cos, sin)
+            value = carry_call([(both, later)], pair)
+        return value, lax.ppermute(later, "gz", to_odd)
+
+    received, sources, scanned, ready = [], [], [], []
+    merged = max(chunks - 2, 0)
+    for c in range(min(2, chunks)):
+        received.append(exchange(pack_call(forward, cotangent, c, shards, received)))
+    for c in range(chunks):
+        before = [sources[-1]] if c else [cos, sin]
+        if merged and c == chunks - 1:
+            ready.append(carry_call(scanned[:merged], own))
+            before.append(ready[0])
+        sources.append(kerr_call(received[c], perm, back, chi_lines, before))
+        scanned.append(scan(sources[-1]))
+        if c + 2 < chunks:
+            before = [received[-1], sources[-1]]
+            received.append(exchange(pack_call(forward, cotangent, c + 2, shards, before)))
+    ready += [carry_call([one], own) for one in scanned[merged:]]
+    return dispersion_call([exchange(array) for array in ready], cos, sin)
 
 
 def solution(mesh):

time: 514 us -> 495 us (0.963)
  waiting for transfers between devices: 186 us -> 90.1 us
  blocking collectives: 0 us -> 50.2 us
  Pallas kernels: 204 us -> 236 us
  local copies, waits for them, and re-layouts: 30.8 us -> 58.3 us
  other arithmetic: 25.6 us -> 2.99 us
  starting transfers between devices: 65.7 us -> 54.1 us
    all_to_all x8 -> x6, waiting for transfers between devices: 148 us -> 62.6 us  [exchange(): return lax.all_to_all(array, 'ma', 0, 0, tiled=True)]
    unnamed x61 -> x81, local copies, waits for them, and re-layouts: 6.52 us -> 42.1 us
    pallas_call x0 -> x15, Pallas kernels: none -> 34.2 us  [the longest x11 29.3 us: carry_call(): pl.pallas_call(carry_kernel, grid=(shards,), out_shape=jax.ShapeDtypeStru...]
    all_to_all x0 -> x1, blocking collectives: none -> 29.4 us  [exchange(): return lax.all_to_all(array, 'ma', 0, 0, tiled=True)]
    all_gather x0 -> x1, blocking collectives: none -> 20.9 us  [on_device(): kept = lax.all_gather(loss[0], 'ma')]
    add x6 -> x0, other arithmetic: 16.6 us -> none  [the longest x4 6.42 us: on_device(): source = cots[c] + lax.all_to_all(kerr, 'ma', 0, 0, tiled=True)]
    all_to_all x8 -> x6, starting transfers between devices: 44.5 us -> 33.2 us  [exchange(): return lax.all_to_all(array, 'ma', 0, 0, tiled=True)]
    ppermute x13, waiting for transfers between devices: 38.4 us -> 27.5 us  [the longest x4 25.6 us: scan(): later = lax.ppermute(value, 'gz', to_chip)]
  transfers between devices with their start and end apart: 21 -> 19, of which waited for: 9 -> 7; matrix products, arithmetic and copies ran while one was open for 6% -> 5% of each run, Pallas kernels for 38% -> 45%
where the time goes in v2:
time: 495 us; the launch traced here: 492 us
  Pallas kernels  236 us (48%)
  waiting for transfers between devices  90.1 us (18%)
  local copies, waits for them, and re-layouts  58.3 us (12%)
  starting transfers between devices  54.1 us (11%)
  blocking collectives  50.2 us (10%)
    pallas_call x4, Pallas kernels, kerr_call(): pl.pallas_call(kerr_kernel, out_shape=jax.ShapeDtypeStruct((shards, 2, lo...  191 us
    all_to_all x6, waiting for transfers between devices, exchange(): return lax.all_to_all(array, 'ma', 0, 0, tiled=True)  62.6 us
    unnamed x81, local copies, waits for them, and re-layouts  42.1 us
    all_to_all x6, starting transfers between devices, exchange(): return lax.all_to_all(array, 'ma', 0, 0, tiled=True)  33.2 us
    all_to_all x1, blocking collectives, exchange(): return lax.all_to_all(array, 'ma', 0, 0, tiled=True)  29.4 us
    pallas_call x11, Pallas kernels, carry_call(): pl.pallas_call(carry_kernel, grid=(shards,), out_shape=jax.ShapeDtypeStru...  29.3 us
    ppermute x4, waiting for transfers between devices, scan(): later = lax.ppermute(value, 'gz', to_chip)  25.6 us
    all_gather x1, blocking collectives, on_device(): kept = lax.all_gather(loss[0], 'ma')  20.9 us
  transfers between devices with their start and end apart: 19, of which 7 were waited for; matrix products, arithmetic and copies ran while one was open for 5% of the time, Pallas kernels for 45%

profile of v2, /device:TPU:0, one launch (start us, length us, event | category | flops | bytes accessed | tf_op | source)
XLA Modules:
  0.0 491.9 jit_solution(4832767380910060467)
XLA Ops:
  7.5 7.3 %all-to-all-start = ((f32[8,4,128,128]{3,2,1,0:T(8,128)}), f32[8,4,128,128]{3,2,1,0:T(8,128)S(1)}, u32[]{:S(2)}, u32[]{:S(2)}) async-start(f32[8,4,128,128]{3,2,1,0:T(8,128)} %pack_chunk.4), calls=%async_computation | async-start | bytes 4194304 | tf_op jit(solution)/shard_map/all_to_all | solution.py:369
  17.7 45.3 %all-to-all-done.x_ref.refs_0_ = f32[8,4,128,128]{3,2,1,0:T(8,128)S(1)} async-done(((f32[8,4,128,128]{3,2,1,0:T(8,128)}), f32[8,4,128,128]{3,2,1,0:T(8,128)S(1)}, u32[]{:S(2)}, u32[]{:S(2)}) %all-to-all-start) | async-done | bytes 2097184 | tf_op jit(solution)/shard_map/all_to_all | solution.py:369
  73.7 9.8 %fusion.2 = (f32[128,4096]{0,1:T(8,128)}, f32[128,4096]{0,1:T(8,128)}) fusion(f32[128,4096]{0,1:T(8,128)} %copy.39), kind=kLoop, calls=%fused_computation.7 | loop fusion | bytes 6291456 | tf_op jit(solution)/shard_map/sin | solution.py:358
  93.0 48.5 %kerr_chunk.4.refs_0_.refs_1_ = f32[8,2,128,128]{3,2,1,0:T(8,128)} custom-call(f32[8,4,128,128]{3,2,1,0:T(8,128)} %copy-done.12, bf16[1024,1024]{1,0:T(8,128)(2,1)} %get-tuple-element.8.perm_ref, bf16[1024,1024]{1,0:T(8,128)(2,1)} %get-tuple-element.7.back_ref, bf16[1024,768]{1,0:T(8,128)(2,1)S(1)} %copy-done.27, bf16[128,96]{1,0:T(8,128)(2,1)S(1)} %copy-done.34, ...), custom_call_target="tpu_custom_call" | custom-call | flops 30000001024 | bytes 12582912 | tf_op jit(solution)/shard_map/kerr_chunk/pallas_call | solution.py:162
  149.8 6.0 %all-to-all-start.3 = ((f32[8,4,128,128]{3,2,1,0:T(8,128)}), f32[8,4,128,128]{3,2,1,0:T(8,128)S(1)}, u32[]{:S(2)}, u32[]{:S(2)}) async-start(f32[8,4,128,128]{3,2,1,0:T(8,128)} %copy-done.10), calls=%async_computation.3 | async-start | bytes 4194304 | tf_op jit(solution)/shard_map/all_to_all | solution.py:369
  158.6 47.5 %kerr_chunk.5.refs_0_.refs_1_ = f32[8,2,128,128]{3,2,1,0:T(8,128)S(1)} custom-call(f32[8,4,128,128]{3,2,1,0:T(8,128)} %copy-done.11, bf16[1024,1024]{1,0:T(8,128)(2,1)} %get-tuple-element.8.perm_ref, bf16[1024,1024]{1,0:T(8,128)(2,1)} %get-tuple-element.7.back_ref, bf16[1024,768]{1,0:T(8,128)(2,1)S(1)} %copy-done.28, bf16[128,96]{1,0:T(8,128)(2,1)S(1)} %copy-done.34, ...), custom_call_target="tpu_custom_call" | custom-call | flops 30000001024 | bytes 12582912 | tf_op jit(solution)/shard_map/kerr_chunk/pallas_call | solution.py:162
  207.4 20.9 %all-gather = f32[8,1,128]{2,1,0:T(1,128)S(1)} all-gather(f32[1,1,128]{2,1,0:T(1,128)S(1)} %bitcast.17), channel_id=1, replica_groups=mesh['gz'=4,'ma'=8] {'ma'}, dimensions={0}, use_global_device_ids=true | all-gather | bytes 4608 | tf_op jit(solution)/shard_map/all_gather | solution.py:363
  228.5 4.2 carry.11.refs_0_
  236.6 12.9 %collective-permute-done.2.refs_1_ = f32[8,2,128,128]{3,2,1,0:T(8,128)} collective-permute-done((f32[8,2,128,128]{3,2,1,0:T(8,128)S(1)}, f32[8,2,128,128]{3,2,1,0:T(8,128)}, u32[]{:S(2)}, u32[]{:S(2)}) %collective-permute-start.2) | collective-permute-done | bytes 1048608 | tf_op jit(solution)/shard_map/ppermute | solution.py:375
  251.9 8.9 %collective-permute-done.5.refs_1_ = f32[8,2,128,128]{3,2,1,0:T(8,128)} collective-permute-done((f32[8,2,128,128]{3,2,1,0:T(8,128)S(1)}, f32[8,2,128,128]{3,2,1,0:T(8,128)}, u32[]{:S(2)}, u32[]{:S(2)}) %collective-permute-start.5) | collective-permute-done | bytes 1048608 | tf_op jit(solution)/shard_map/ppermute | solution.py:375
  271.4 4.4 all-to-all-start.5
  279.8 47.6 %kerr_chunk.6.refs_0_ = f32[8,2,128,128]{3,2,1,0:T(8,128)S(1)} custom-call(f32[8,4,128,128]{3,2,1,0:T(8,128)} %copy-done.8, bf16[1024,1024]{1,0:T(8,128)(2,1)} %get-tuple-element.8.perm_ref, bf16[1024,1024]{1,0:T(8,128)(2,1)} %get-tuple-element.7.back_ref, bf16[1024,768]{1,0:T(8,128)(2,1)S(1)} %copy-done.29, bf16[128,96]{1,0:T(8,128)(2,1)S(1)} %copy-done.34, ...), custom_call_target="tpu_custom_call" | custom-call | flops 30000001024 | bytes 12582912 | tf_op jit(solution)/shard_map/kerr_chunk/pallas_call | solution.py:162
  332.2 3.9 carry.12.refs_0_
  336.2 3.8 carry.14.refs_2_
  340.0 5.8 %carry.15.refs_1_ = f32[8,4,128,128]{3,2,1,0:T(8,128)} custom-call(f32[8,128,128]{2,1,0:T(8,128)S(1)} %broadcast_in_dim.16.factor_ref, f32[8,2,128,128]{3,2,1,0:T(8,128)S(1)} %carry.12.refs_0_, f32[8,2,128,128]{3,2,1,0:T(8,128)} %collective-permute-done.3.refs_1_, f32[8,2,128,128]{3,2,1,0:T(8,128)S(1)} %carry.14.refs_2_, ...), custom_call_target="tpu_custom_call" | custom-call | bytes 6291456 | tf_op jit(solution)/shard_map/carry/pallas_call | solution.py:218
  347.4 5.9 %all-to-all-start.2 = ((f32[8,4,128,128]{3,2,1,0:T(8,128)}), f32[8,4,128,128]{3,2,1,0:T(8,128)}, u32[]{:S(2)}, u32[]{:S(2)}) async-start(f32[8,4,128,128]{3,2,1,0:T(8,128)} %carry.15.refs_1_), calls=%async_computation.2 | async-start | bytes 4194304 | tf_op jit(solution)/shard_map/all_to_all | solution.py:369
  356.1 47.5 %kerr_chunk.7.refs_0_ = f32[8,2,128,128]{3,2,1,0:T(8,128)S(1)} custom-call(f32[8,4,128,128]{3,2,1,0:T(8,128)} %all-to-all-done.5.x_ref, bf16[1024,1024]{1,0:T(8,128)(2,1)} %get-tuple-element.8.perm_ref, bf16[1024,1024]{1,0:T(8,128)(2,1)} %get-tuple-element.7.back_ref, bf16[1024,768]{1,0:T(8,128)(2,1)S(1)} %copy-done.30, bf16[128,96]{1,0:T(8,128)(2,1)S(1)} %copy-done.34, ...), custom_call_target="tpu_custom_call" | custom-call | flops 30000001024 | bytes 12582912 | tf_op jit(solution)/shard_map/kerr_chunk/pallas_call | solution.py:162
  409.7 3.8 carry.17.refs_0_
  416.4 6.0 %all-to-all-start.4 = ((f32[8,2,128,128]{3,2,1,0:T(8,128)}), f32[8,2,128,128]{3,2,1,0:T(8,128)}, u32[]{:S(2)}, u32[]{:S(2)}) async-start(f32[8,2,128,128]{3,2,1,0:T(8,128)} %carry.18), calls=%async_computation.4 | async-start | bytes 2097152 | tf_op jit(solution)/shard_map/all_to_all | solution.py:369
  422.4 3.8 collective-permute-done.11.refs_1_
  427.5 3.8 carry.20.refs_0_
  431.7 17.2 %all-to-all-done.4.refs_1_ = f32[8,2,128,128]{3,2,1,0:T(8,128)} async-done(((f32[8,2,128,128]{3,2,1,0:T(8,128)}), f32[8,2,128,128]{3,2,1,0:T(8,128)}, u32[]{:S(2)}, u32[]{:S(2)}) %all-to-all-start.4) | async-done | bytes 1048608 | tf_op jit(solution)/shard_map/all_to_all | solution.py:369
  448.9 29.4 %all_to_all.35.refs_2_ = f32[8,2,128,128]{3,2,1,0:T(8,128)S(1)} all-to-all(f32[8,2,128,128]{3,2,1,0:T(8,128)S(1)} %carry.21), channel_id=1, replica_groups=mesh['gz'=4,'ma'=8] {'ma'}, dimensions={0} | all-to-all | bytes 2097152 | tf_op jit(solution)/shard_map/all_to_all | solution.py:369
  481.5 10.4 %dispersion.1 = f32[1,2,128,4096]{3,2,1,0:T(8,128)} custom-call(f32[8,4,128,128]{3,2,1,0:T(8,128)} %all-to-all-done.2.refs_0_, f32[8,2,128,128]{3,2,1,0:T(8,128)} %all-to-all-done.4.refs_1_, f32[8,2,128,128]{3,2,1,0:T(8,128)S(1)} %all_to_all.35.refs_2_, f32[32,128,128]{2,1,0:T(8,128)S(1)} %bitcast.10, f32[32,128,128]{2,1,0:T(8,128)S(1)} %bitcast.8, ...), custom_call_target="tpu_custom_call" | custom-call | flops 4000000000 | bytes 16777216 | tf_op jit(solution)/shard_map/dispersion/pallas_call | solution.py:323
  (127 shorter events, 86.8 us)
Async XLA Ops:
  7.5 55.5 %all-to-all-start = ((f32[8,4,128,128]{3,2,1,0:T(8,128)}), f32[8,4,128,128]{3,2,1,0:T(8,128)S(1)}, u32[]{:S(2)}, u32[]{:S(2)}) async-start(f32[8,4,128,128]{3,2,1,0:T(8,128)} %pack_chunk.4), calls=%async_computation | async-start | bytes 4194304 | tf_op jit(solution)/shard_map/all_to_all | solution.py:369
  70.1 72.7 %all-to-all-start.1 = ((f32[8,4,128,128]{3,2,1,0:T(8,128)}), f32[8,4,128,128]{3,2,1,0:T(8,128)S(1)}, u32[]{:S(2)}, u32[]{:S(2)}) async-start(f32[8,4,128,128]{3,2,1,0:T(8,128)} %copy-done.13), calls=%async_computation.1 | async-start | bytes 4194304 | tf_op jit(solution)/shard_map/all_to_all | solution.py:369
  141.5 86.8 %collective-permute-start.1 = (f32[8,2,128,128]{3,2,1,0:T(8,128)}, f32[8,2,128,128]{3,2,1,0:T(8,128)}, u32[]{:S(2)}, u32[]{:S(2)}) collective-permute-start(f32[8,2,128,128]{3,2,1,0:T(8,128)} %kerr_chunk.4.refs_0_.refs_1_), channel_id=1, source_target_pairs={{8,0},{24,16},{9,1},{25,17},{10,2},{26,18},{11,3},{27,19},{12,4},{... | collective-permute-start | bytes 3145736 | tf_op jit(solution)/shard_map/ppermute | solution.py:372
  149.8 113.3 %all-to-all-start.3 = ((f32[8,4,128,128]{3,2,1,0:T(8,128)}), f32[8,4,128,128]{3,2,1,0:T(8,128)S(1)}, u32[]{:S(2)}, u32[]{:S(2)}) async-start(f32[8,4,128,128]{3,2,1,0:T(8,128)} %copy-done.10), calls=%async_computation.3 | async-start | bytes 4194304 | tf_op jit(solution)/shard_map/all_to_all | solution.py:369
  158.6 48.8 %copy-start.39 = (f32[1,128]{1,0:T(1,128)S(1)}, f32[1,128]{1,0:T(1,128)}, u32[]{:S(2)}) copy-start(f32[1,128]{1,0:T(1,128)} %param.32) | copy-start | bytes 1540
  206.1 27.9 %collective-permute-start.4 = (f32[8,2,128,128]{3,2,1,0:T(8,128)S(1)}, f32[8,2,128,128]{3,2,1,0:T(8,128)S(1)}, u32[]{:S(2)}, u32[]{:S(2)}) collective-permute-start(f32[8,2,128,128]{3,2,1,0:T(8,128)S(1)} %kerr_chunk.5.refs_0_.refs_1_), channel_id=1, source_target_pairs={{8,0},{24,16},{9,1},{25,17},{10,2},{26,18},{11,3},{27,19},{12,4},{... | collective-permute-start | bytes 3145736 | tf_op jit(solution)/shard_map/ppermute | solution.py:372
  232.7 16.8 %collective-permute-start.2 = (f32[8,2,128,128]{3,2,1,0:T(8,128)S(1)}, f32[8,2,128,128]{3,2,1,0:T(8,128)}, u32[]{:S(2)}, u32[]{:S(2)}) collective-permute-start(f32[8,2,128,128]{3,2,1,0:T(8,128)S(1)} %carry.11.refs_0_), channel_id=1, source_target_pairs={{16,0},{17,1},{18,2},{19,3},{20,4},{21,5},{22,6},{23,7}} | collective-permute-start | bytes 3145736 | tf_op jit(solution)/shard_map/ppermute | solution.py:375
  234.3 26.4 %collective-permute-start.5 = (f32[8,2,128,128]{3,2,1,0:T(8,128)S(1)}, f32[8,2,128,128]{3,2,1,0:T(8,128)}, u32[]{:S(2)}, u32[]{:S(2)}) collective-permute-start(f32[8,2,128,128]{3,2,1,0:T(8,128)S(1)} %carry.13.refs_0_), channel_id=1, source_target_pairs={{16,0},{17,1},{18,2},{19,3},{20,4},{21,5},{22,6},{23,7}} | collective-permute-start | bytes 3145736 | tf_op jit(solution)/shard_map/ppermute | solution.py:375
  249.5 90.5 %collective-permute-start.3 = (f32[8,2,128,128]{3,2,1,0:T(8,128)}, f32[8,2,128,128]{3,2,1,0:T(8,128)}, u32[]{:S(2)}, u32[]{:S(2)}) collective-permute-start(f32[8,2,128,128]{3,2,1,0:T(8,128)} %collective-permute-done.2.refs_1_), channel_id=1, source_target_pairs={{0,8},{16,24},{1,9},{17,25},{2,10},{18,26},{3,11},{19,27},{4,12},{... | collective-permute-start | bytes 3145736 | tf_op jit(solution)/shard_map/ppermute | solution.py:377
  260.8 79.3 %collective-permute-start.6 = (f32[8,2,128,128]{3,2,1,0:T(8,128)}, f32[8,2,128,128]{3,2,1,0:T(8,128)}, u32[]{:S(2)}, u32[]{:S(2)}) collective-permute-start(f32[8,2,128,128]{3,2,1,0:T(8,128)} %collective-permute-done.5.refs_1_), channel_id=1, source_target_pairs={{0,8},{16,24},{1,9},{17,25},{2,10},{18,26},{3,11},{19,27},{4,12},{... | collective-permute-start | bytes 3145736 | tf_op jit(solution)/shard_map/ppermute | solution.py:377
  271.4 76.0 %all-to-all-start.5 = ((f32[8,4,128,128]{3,2,1,0:T(8,128)}), f32[8,4,128,128]{3,2,1,0:T(8,128)}, u32[]{:S(2)}, u32[]{:S(2)}) async-start(f32[8,4,128,128]{3,2,1,0:T(8,128)} %copy-done.9), calls=%async_computation.5 | async-start | bytes 4194304 | tf_op jit(solution)/shard_map/all_to_all | solution.py:369
  279.8 52.4 %copy-start.15 = (f32[8,2,128,128]{3,2,1,0:T(8,128)S(1)}, f32[8,2,128,128]{3,2,1,0:T(8,128)}, u32[]{:S(2)}) copy-start(f32[8,2,128,128]{3,2,1,0:T(8,128)} %copy-done.14) | copy-start | bytes 3145732
  327.4 18.4 %collective-permute-start.7 = (f32[8,2,128,128]{3,2,1,0:T(8,128)S(1)}, f32[8,2,128,128]{3,2,1,0:T(8,128)S(1)}, u32[]{:S(2)}, u32[]{:S(2)}) collective-permute-start(f32[8,2,128,128]{3,2,1,0:T(8,128)S(1)} %kerr_chunk.6.refs_0_), channel_id=1, source_target_pairs={{8,0},{24,16},{9,1},{25,17},{10,2},{26,18},{11,3},{27,19},{12,4},{... | collective-permute-start | bytes 3145736 | tf_op jit(solution)/shard_map/ppermute | solution.py:372
  328.9 3.1 collective-permute-start
  346.1 58.8 %collective-permute-start.8 = (f32[8,2,128,128]{3,2,1,0:T(8,128)S(1)}, f32[8,2,128,128]{3,2,1,0:T(8,128)}, u32[]{:S(2)}, u32[]{:S(2)}) collective-permute-start(f32[8,2,128,128]{3,2,1,0:T(8,128)S(1)} %carry.16.refs_0_), channel_id=1, source_target_pairs={{16,0},{17,1},{18,2},{19,3},{20,4},{21,5},{22,6},{23,7}} | collective-permute-start | bytes 3145736 | tf_op jit(solution)/shard_map/ppermute | solution.py:375
  347.4 69.0 %all-to-all-start.2 = ((f32[8,4,128,128]{3,2,1,0:T(8,128)}), f32[8,4,128,128]{3,2,1,0:T(8,128)}, u32[]{:S(2)}, u32[]{:S(2)}) async-start(f32[8,4,128,128]{3,2,1,0:T(8,128)} %carry.15.refs_1_), calls=%async_computation.2 | async-start | bytes 4194304 | tf_op jit(solution)/shard_map/all_to_all | solution.py:369
  403.6 4.6 collective-permute-start.10
  404.9 8.6 %collective-permute-start.9 = (f32[8,2,128,128]{3,2,1,0:T(8,128)}, f32[8,2,128,128]{3,2,1,0:T(8,128)S(1)}, u32[]{:S(2)}, u32[]{:S(2)}) collective-permute-start(f32[8,2,128,128]{3,2,1,0:T(8,128)} %collective-permute-done.8.refs_1_), channel_id=1, source_target_pairs={{0,8},{16,24},{1,9},{17,25},{2,10},{18,26},{3,11},{19,27},{4,12},{... | collective-permute-start | bytes 3145736 | tf_op jit(solution)/shard_map/ppermute | solution.py:377
  408.4 17.8 %collective-permute-start.11 = (f32[8,2,128,128]{3,2,1,0:T(8,128)S(1)}, f32[8,2,128,128]{3,2,1,0:T(8,128)}, u32[]{:S(2)}, u32[]{:S(2)}) collective-permute-start(f32[8,2,128,128]{3,2,1,0:T(8,128)S(1)} %carry.19.refs_0_), channel_id=1, source_target_pairs={{16,0},{17,1},{18,2},{19,3},{20,4},{21,5},{22,6},{23,7}} | collective-permute-start | bytes 3145736 | tf_op jit(solution)/shard_map/ppermute | solution.py:375
  416.4 32.5 %all-to-all-start.4 = ((f32[8,2,128,128]{3,2,1,0:T(8,128)}), f32[8,2,128,128]{3,2,1,0:T(8,128)}, u32[]{:S(2)}, u32[]{:S(2)}) async-start(f32[8,2,128,128]{3,2,1,0:T(8,128)} %carry.18), calls=%async_computation.4 | async-start | bytes 2097152 | tf_op jit(solution)/shard_map/all_to_all | solution.py:369
  426.2 5.2 %collective-permute-start.12 = (f32[8,2,128,128]{3,2,1,0:T(8,128)}, f32[8,2,128,128]{3,2,1,0:T(8,128)S(1)}, u32[]{:S(2)}, u32[]{:S(2)}) collective-permute-start(f32[8,2,128,128]{3,2,1,0:T(8,128)} %collective-permute-done.11.refs_1_), channel_id=1, source_target_pairs={{0,8},{16,24},{1,9},{17,25},{2,10},{18,26},{3,11},{19,27},{4,12},{... | collective-permute-start | bytes 3145736 | tf_op jit(solution)/shard_map/ppermute | solution.py:377
  431.4 46.9 %copy-start.31 = (bf16[768,256]{1,0:T(8,128)(2,1)S(1)}, bf16[768,256]{1,0:T(8,128)(2,1)}, u32[]{:S(2)}) copy-start(bf16[768,256]{1,0:T(8,128)(2,1)} %constant.24.clone.refs_7_) | copy-start | bytes 1179652
  431.4 46.9 %copy-start.32 = (bf16[768,256]{1,0:T(8,128)(2,1)S(1)}, bf16[768,256]{1,0:T(8,128)(2,1)}, u32[]{:S(2)}) copy-start(bf16[768,256]{1,0:T(8,128)(2,1)} %constant.23.clone.refs_6_) | copy-start | bytes 1179652
  431.4 46.9 %copy-start.33 = (f32[2,32,128]{2,1,0:T(8,128)S(1)}, f32[2,32,128]{2,1,0:T(8,128)}, u32[]{:S(2)}) copy-start(f32[2,32,128]{2,1,0:T(8,128)} %constant.22.clone.refs_5_) | copy-start | bytes 98308
  (35 other events, 128.7 us)

commit v3 on v2

--- a/solution.py
+++ b/solution.py
@@ -176,7 +176,7 @@
         ],
         compiler_params=pltpu.CompilerParams(vmem_limit_bytes=48 << 20),
         cost_estimate=pl.CostEstimate(
-            flops=30_000_000_000, bytes_accessed=12 << 20, transcendentals=0
+            flops=56_000_000_000, bytes_accessed=12 << 20, transcendentals=0
         ),
         name="kerr_chunk",
     )(*operands, *before)
@@ -379,7 +379,8 @@
     received, sources, scanned, ready = [], [], [], []
     merged = max(chunks - 2, 0)
     for c in range(min(2, chunks)):
-        received.append(exchange(pack_call(forward, cotangent, c, shards, received)))
+        before = received + [cos, sin, perm, back, chi_lines, own, pair] * c
+        received.append(exchange(pack_call(forward, cotangent, c, shards, before)))
     for c in range(chunks):
         before = [sources[-1]] if c else [cos, sin]
         if merged and c == chunks - 1:

time: 495 us -> 487 us (0.984)
  waiting for transfers between devices: 90.1 us -> 42 us
  blocking collectives: 50.2 us -> 79.1 us
  starting transfers between devices: 54.1 us -> 62.8 us
    all_to_all x6, waiting for transfers between devices: 62.6 us -> 16.3 us  [exchange(): return lax.all_to_all(array, 'ma', 0, 0, tiled=True)]
    all_gather x1, blocking collectives: 20.9 us -> 49.5 us  [on_device(): kept = lax.all_gather(loss[0], 'ma')]
    all_to_all x6, starting transfers between devices: 33.2 us -> 41.9 us  [exchange(): return lax.all_to_all(array, 'ma', 0, 0, tiled=True)]
    unnamed x81 -> x93, local copies, waits for them, and re-layouts: 42.1 us -> 46.2 us
  transfers between devices with their start and end apart: 19 -> 19, of which waited for: 7 -> 5; matrix products, arithmetic and copies ran while one was open for 5% -> 4% of each run, Pallas kernels for 45% -> 46%
where the time goes in v3:
time: 487 us; the launch traced here: 484 us
  Pallas kernels  236 us (48%)
  blocking collectives  79.1 us (16%)
  starting transfers between devices  62.8 us (13%)
  local copies, waits for them, and re-layouts  60.6 us (12%)
  waiting for transfers between devices  42 us (9%)
    pallas_call x4, Pallas kernels, kerr_call(): pl.pallas_call(kerr_kernel, out_shape=jax.ShapeDtypeStruct((shards, 2, lo...  191 us
    all_gather x1, blocking collectives, on_device(): kept = lax.all_gather(loss[0], 'ma')  49.5 us
    unnamed x93, local copies, waits for them, and re-layouts  46.2 us
    all_to_all x6, starting transfers between devices, exchange(): return lax.all_to_all(array, 'ma', 0, 0, tiled=True)  41.9 us
    all_to_all x1, blocking collectives, exchange(): return lax.all_to_all(array, 'ma', 0, 0, tiled=True)  29.7 us
    pallas_call x11, Pallas kernels, carry_call(): pl.pallas_call(carry_kernel, grid=(shards,), out_shape=jax.ShapeDtypeStru...  29.2 us
    ppermute x4, waiting for transfers between devices, scan(): later = lax.ppermute(value, 'gz', to_chip)  25.6 us
    all_to_all x6, waiting for transfers between devices, exchange(): return lax.all_to_all(array, 'ma', 0, 0, tiled=True)  16.3 us
  transfers between devices with their start and end apart: 19, of which 5 were waited for; matrix products, arithmetic and copies ran while one was open for 4% of the time, Pallas kernels for 46%

profile of v3, /device:TPU:0, one launch (start us, length us, event | category | flops | bytes accessed | tf_op | source)
XLA Modules:
  0.0 483.8 jit_solution(14410053976744047024)
XLA Ops:
  7.5 7.4 %all-to-all-start = ((f32[8,4,128,128]{3,2,1,0:T(8,128)}), f32[8,4,128,128]{3,2,1,0:T(8,128)}, u32[]{:S(2)}, u32[]{:S(2)}) async-start(f32[8,4,128,128]{3,2,1,0:T(8,128)} %pack_chunk.4), calls=%async_computation | async-start | bytes 4194304 | tf_op jit(solution)/shard_map/all_to_all | solution.py:369
  15.0 49.5 %all-gather = f32[8,1,128]{2,1,0:T(1,128)S(1)} all-gather(f32[1,1,128]{2,1,0:T(1,128)S(1)} %bitcast.19), channel_id=1, replica_groups=mesh['gz'=4,'ma'=8] {'ma'}, dimensions={0}, use_global_device_ids=true | all-gather | bytes 4608 | tf_op jit(solution)/shard_map/all_gather | solution.py:363
  70.8 8.2 %fusion.2 = (f32[128,4096]{0,1:T(8,128)}, f32[128,4096]{0,1:T(8,128)}) fusion(f32[128,4096]{0,1:T(8,128)S(1)} %copy.39), kind=kLoop, calls=%fused_computation.7 | loop fusion | bytes 6291456 | tf_op jit(solution)/shard_map/sin | solution.py:358
  97.0 10.6 %all-to-all-start.1 = ((f32[8,4,128,128]{3,2,1,0:T(8,128)}), f32[8,4,128,128]{3,2,1,0:T(8,128)S(1)}, u32[]{:S(2)}, u32[]{:S(2)}) async-start(f32[8,4,128,128]{3,2,1,0:T(8,128)} %copy-done.20), calls=%async_computation.1 | async-start | bytes 4194304 | tf_op jit(solution)/shard_map/all_to_all | solution.py:369
  110.4 48.5 %kerr_chunk.4.refs_0_.refs_1_ = f32[8,2,128,128]{3,2,1,0:T(8,128)} custom-call(f32[8,4,128,128]{3,2,1,0:T(8,128)} %all-to-all-done.x_ref.refs_0_, bf16[1024,1024]{1,0:T(8,128)(2,1)} %get-tuple-element.8.perm_ref.refs_3_, bf16[1024,1024]{1,0:T(8,128)(2,1)} %get-tuple-element.7.back_ref.refs_4_, bf16[1024,768]{1,0:T(8,128)(2,1)S(1)} %copy-done.29, ...), custom_call_target="tpu_custom_call" | custom-call | flops 56000000000 | bytes 12582912 | tf_op jit(solution)/shard_map/kerr_chunk/pallas_call | solution.py:162
  167.2 6.0 %all-to-all-start.3 = ((f32[8,4,128,128]{3,2,1,0:T(8,128)}), f32[8,4,128,128]{3,2,1,0:T(8,128)S(1)}, u32[]{:S(2)}, u32[]{:S(2)}) async-start(f32[8,4,128,128]{3,2,1,0:T(8,128)} %copy-done.11), calls=%async_computation.3 | async-start | bytes 4194304 | tf_op jit(solution)/shard_map/all_to_all | solution.py:369
  176.0 47.5 %kerr_chunk.5.refs_0_.refs_1_ = f32[8,2,128,128]{3,2,1,0:T(8,128)S(1)} custom-call(f32[8,4,128,128]{3,2,1,0:T(8,128)} %copy-done.13, bf16[1024,1024]{1,0:T(8,128)(2,1)} %get-tuple-element.8.perm_ref.refs_3_, bf16[1024,1024]{1,0:T(8,128)(2,1)} %get-tuple-element.7.back_ref.refs_4_, bf16[1024,768]{1,0:T(8,128)(2,1)S(1)} %copy-done.30, ...), custom_call_target="tpu_custom_call" | custom-call | flops 56000000000 | bytes 12582912 | tf_op jit(solution)/shard_map/kerr_chunk/pallas_call | solution.py:162
  224.9 4.2 carry.11.refs_0_
  233.0 12.9 %collective-permute-done.2.refs_1_ = f32[8,2,128,128]{3,2,1,0:T(8,128)} collective-permute-done((f32[8,2,128,128]{3,2,1,0:T(8,128)S(1)}, f32[8,2,128,128]{3,2,1,0:T(8,128)}, u32[]{:S(2)}, u32[]{:S(2)}) %collective-permute-start.2) | collective-permute-done | bytes 1048608 | tf_op jit(solution)/shard_map/ppermute | solution.py:375
  248.2 8.9 %collective-permute-done.5.refs_1_ = f32[8,2,128,128]{3,2,1,0:T(8,128)} collective-permute-done((f32[8,2,128,128]{3,2,1,0:T(8,128)S(1)}, f32[8,2,128,128]{3,2,1,0:T(8,128)}, u32[]{:S(2)}, u32[]{:S(2)}) %collective-permute-start.5) | collective-permute-done | bytes 1048608 | tf_op jit(solution)/shard_map/ppermute | solution.py:375
  267.8 6.0 %all-to-all-start.5 = ((f32[8,4,128,128]{3,2,1,0:T(8,128)}), f32[8,4,128,128]{3,2,1,0:T(8,128)}, u32[]{:S(2)}, u32[]{:S(2)}) async-start(f32[8,4,128,128]{3,2,1,0:T(8,128)} %copy-done.12), calls=%async_computation.5 | async-start | bytes 4194304 | tf_op jit(solution)/shard_map/all_to_all | solution.py:369
  277.8 47.6 %kerr_chunk.6.refs_0_ = f32[8,2,128,128]{3,2,1,0:T(8,128)S(1)} custom-call(f32[8,4,128,128]{3,2,1,0:T(8,128)} %copy-done.10, bf16[1024,1024]{1,0:T(8,128)(2,1)} %get-tuple-element.8.perm_ref.refs_3_, bf16[1024,1024]{1,0:T(8,128)(2,1)} %get-tuple-element.7.back_ref.refs_4_, bf16[1024,768]{1,0:T(8,128)(2,1)S(1)} %copy-done.31, bf16[128,96]{1,0:T(8,128)(2,1)S(1)} %copy-done.40, ...), custom_call_target="tpu_custom_call" | custom-call | flops 56000000000 | bytes 12582912 | tf_op jit(solution)/shard_map/kerr_chunk/pallas_call | solution.py:162
  326.9 3.8 carry.12.refs_0_
  330.7 3.8 carry.14.refs_2_
  334.6 5.8 %carry.15.refs_1_ = f32[8,4,128,128]{3,2,1,0:T(8,128)} custom-call(f32[8,128,128]{2,1,0:T(8,128)S(1)} %broadcast_in_dim.16.factor_ref.refs_6_, f32[8,2,128,128]{3,2,1,0:T(8,128)S(1)} %carry.12.refs_0_, f32[8,2,128,128]{3,2,1,0:T(8,128)} %collective-permute-done.3.refs_1_, f32[8,2,128,128]{3,2,1,0:T(8,128)S(1)} %carry.14.refs_2_, ...), custom_call_target="tpu_custom_call" | custom-call | bytes 6291456 | tf_op jit(solution)/shard_map/carry/pallas_call | solution.py:218
  342.0 6.0 %all-to-all-start.2 = ((f32[8,4,128,128]{3,2,1,0:T(8,128)}), f32[8,4,128,128]{3,2,1,0:T(8,128)}, u32[]{:S(2)}, u32[]{:S(2)}) async-start(f32[8,4,128,128]{3,2,1,0:T(8,128)} %carry.15.refs_1_), calls=%async_computation.2 | async-start | bytes 4194304 | tf_op jit(solution)/shard_map/all_to_all | solution.py:369
  350.8 47.5 %kerr_chunk.7.refs_0_ = f32[8,2,128,128]{3,2,1,0:T(8,128)S(1)} custom-call(f32[8,4,128,128]{3,2,1,0:T(8,128)} %all-to-all-done.5.x_ref, bf16[1024,1024]{1,0:T(8,128)(2,1)} %get-tuple-element.8.perm_ref.refs_3_, bf16[1024,1024]{1,0:T(8,128)(2,1)} %get-tuple-element.7.back_ref.refs_4_, bf16[1024,768]{1,0:T(8,128)(2,1)S(1)} %copy-done.32, ...), custom_call_target="tpu_custom_call" | custom-call | flops 56000000000 | bytes 12582912 | tf_op jit(solution)/shard_map/kerr_chunk/pallas_call | solution.py:162
  404.5 3.8 carry.17.refs_0_
  411.2 5.9 %all-to-all-start.4 = ((f32[8,2,128,128]{3,2,1,0:T(8,128)}), f32[8,2,128,128]{3,2,1,0:T(8,128)}, u32[]{:S(2)}, u32[]{:S(2)}) async-start(f32[8,2,128,128]{3,2,1,0:T(8,128)} %carry.18), calls=%async_computation.4 | async-start | bytes 2097152 | tf_op jit(solution)/shard_map/all_to_all | solution.py:369
  417.1 3.8 collective-permute-done.11.refs_1_
  422.2 3.8 carry.20.refs_0_
  427.4 16.2 %all-to-all-done.4.refs_1_ = f32[8,2,128,128]{3,2,1,0:T(8,128)} async-done(((f32[8,2,128,128]{3,2,1,0:T(8,128)}), f32[8,2,128,128]{3,2,1,0:T(8,128)}, u32[]{:S(2)}, u32[]{:S(2)}) %all-to-all-start.4) | async-done | bytes 1048608 | tf_op jit(solution)/shard_map/all_to_all | solution.py:369
  443.6 29.7 %all_to_all.35.refs_2_ = f32[8,2,128,128]{3,2,1,0:T(8,128)S(1)} all-to-all(f32[8,2,128,128]{3,2,1,0:T(8,128)} %copy-done.25), channel_id=1, replica_groups=mesh['gz'=4,'ma'=8] {'ma'}, dimensions={0} | all-to-all | bytes 2097152 | tf_op jit(solution)/shard_map/all_to_all | solution.py:369
  473.3 10.4 %dispersion.1 = f32[1,2,128,4096]{3,2,1,0:T(8,128)} custom-call(f32[8,4,128,128]{3,2,1,0:T(8,128)} %all-to-all-done.2.refs_0_, f32[8,2,128,128]{3,2,1,0:T(8,128)} %all-to-all-done.4.refs_1_, f32[8,2,128,128]{3,2,1,0:T(8,128)S(1)} %all_to_all.35.refs_2_, f32[32,128,128]{2,1,0:T(8,128)S(1)} %bitcast.9, f32[32,128,128]{2,1,0:T(8,128)S(1)} %bitcast.12, ...), custom_call_target="tpu_custom_call" | custom-call | flops 4000000000 | bytes 16777216 | tf_op jit(solution)/shard_map/dispersion/pallas_call | solution.py:323
  (139 shorter events, 85.2 us)
Async XLA Ops:
  7.5 58.2 %copy-start.42 = (s32[128,128]{1,0:T(8,128)S(1)}, s32[128,128]{1,0:T(8,128)}, u32[]{:S(2)}) copy-start(s32[128,128]{1,0:T(8,128)} %param.29) | copy-start | bytes 196612
  7.5 77.2 %all-to-all-start = ((f32[8,4,128,128]{3,2,1,0:T(8,128)}), f32[8,4,128,128]{3,2,1,0:T(8,128)}, u32[]{:S(2)}, u32[]{:S(2)}) async-start(f32[8,4,128,128]{3,2,1,0:T(8,128)} %pack_chunk.4), calls=%async_computation | async-start | bytes 4194304 | tf_op jit(solution)/shard_map/all_to_all | solution.py:369
  64.4 20.3 %collective-permute-start = (f32[8,128]{1,0:T(8,128)S(1)}, f32[8,128]{1,0:T(8,128)S(1)}, u32[]{:S(2)}, u32[]{:S(2)}) collective-permute-start(f32[8,128]{1,0:T(8,128)S(1)} %bitcast.16), channel_id=1, source_target_pairs={{8,0},{24,16},{9,1},{25,17},{10,2},{26,18},{11,3},{27,19},{12,4},{... | collective-permute-start | bytes 12296 | tf_op jit(solution)/shard_map/ppermute | solution.py:366
  97.0 63.2 %all-to-all-start.1 = ((f32[8,4,128,128]{3,2,1,0:T(8,128)}), f32[8,4,128,128]{3,2,1,0:T(8,128)S(1)}, u32[]{:S(2)}, u32[]{:S(2)}) async-start(f32[8,4,128,128]{3,2,1,0:T(8,128)} %copy-done.20), calls=%async_computation.1 | async-start | bytes 4194304 | tf_op jit(solution)/shard_map/all_to_all | solution.py:369
  158.9 65.9 %collective-permute-start.1 = (f32[8,2,128,128]{3,2,1,0:T(8,128)}, f32[8,2,128,128]{3,2,1,0:T(8,128)}, u32[]{:S(2)}, u32[]{:S(2)}) collective-permute-start(f32[8,2,128,128]{3,2,1,0:T(8,128)} %kerr_chunk.4.refs_0_.refs_1_), channel_id=1, source_target_pairs={{8,0},{24,16},{9,1},{25,17},{10,2},{26,18},{11,3},{27,19},{12,4},{... | collective-permute-start | bytes 3145736 | tf_op jit(solution)/shard_map/ppermute | solution.py:372
  167.2 92.2 %all-to-all-start.3 = ((f32[8,4,128,128]{3,2,1,0:T(8,128)}), f32[8,4,128,128]{3,2,1,0:T(8,128)S(1)}, u32[]{:S(2)}, u32[]{:S(2)}) async-start(f32[8,4,128,128]{3,2,1,0:T(8,128)} %copy-done.11), calls=%async_computation.3 | async-start | bytes 4194304 | tf_op jit(solution)/shard_map/all_to_all | solution.py:369
  223.6 6.8 %collective-permute-start.4 = (f32[8,2,128,128]{3,2,1,0:T(8,128)S(1)}, f32[8,2,128,128]{3,2,1,0:T(8,128)S(1)}, u32[]{:S(2)}, u32[]{:S(2)}) collective-permute-start(f32[8,2,128,128]{3,2,1,0:T(8,128)S(1)} %kerr_chunk.5.refs_0_.refs_1_), channel_id=1, source_target_pairs={{8,0},{24,16},{9,1},{25,17},{10,2},{26,18},{11,3},{27,19},{12,4},{... | collective-permute-start | bytes 3145736 | tf_op jit(solution)/shard_map/ppermute | solution.py:372
  229.1 16.8 %collective-permute-start.2 = (f32[8,2,128,128]{3,2,1,0:T(8,128)S(1)}, f32[8,2,128,128]{3,2,1,0:T(8,128)}, u32[]{:S(2)}, u32[]{:S(2)}) collective-permute-start(f32[8,2,128,128]{3,2,1,0:T(8,128)S(1)} %carry.11.refs_0_), channel_id=1, source_target_pairs={{16,0},{17,1},{18,2},{19,3},{20,4},{21,5},{22,6},{23,7}} | collective-permute-start | bytes 3145736 | tf_op jit(solution)/shard_map/ppermute | solution.py:375
  230.7 26.4 %collective-permute-start.5 = (f32[8,2,128,128]{3,2,1,0:T(8,128)S(1)}, f32[8,2,128,128]{3,2,1,0:T(8,128)}, u32[]{:S(2)}, u32[]{:S(2)}) collective-permute-start(f32[8,2,128,128]{3,2,1,0:T(8,128)S(1)} %carry.13.refs_0_), channel_id=1, source_target_pairs={{16,0},{17,1},{18,2},{19,3},{20,4},{21,5},{22,6},{23,7}} | collective-permute-start | bytes 3145736 | tf_op jit(solution)/shard_map/ppermute | solution.py:375
  245.9 88.7 %collective-permute-start.3 = (f32[8,2,128,128]{3,2,1,0:T(8,128)}, f32[8,2,128,128]{3,2,1,0:T(8,128)}, u32[]{:S(2)}, u32[]{:S(2)}) collective-permute-start(f32[8,2,128,128]{3,2,1,0:T(8,128)} %collective-permute-done.2.refs_1_), channel_id=1, source_target_pairs={{0,8},{16,24},{1,9},{17,25},{2,10},{18,26},{3,11},{19,27},{4,12},{... | collective-permute-start | bytes 3145736 | tf_op jit(solution)/shard_map/ppermute | solution.py:377
  257.1 77.5 %collective-permute-start.6 = (f32[8,2,128,128]{3,2,1,0:T(8,128)}, f32[8,2,128,128]{3,2,1,0:T(8,128)}, u32[]{:S(2)}, u32[]{:S(2)}) collective-permute-start(f32[8,2,128,128]{3,2,1,0:T(8,128)} %collective-permute-done.5.refs_1_), channel_id=1, source_target_pairs={{0,8},{16,24},{1,9},{17,25},{2,10},{18,26},{3,11},{19,27},{4,12},{... | collective-permute-start | bytes 3145736 | tf_op jit(solution)/shard_map/ppermute | solution.py:377
  267.8 74.2 %all-to-all-start.5 = ((f32[8,4,128,128]{3,2,1,0:T(8,128)}), f32[8,4,128,128]{3,2,1,0:T(8,128)}, u32[]{:S(2)}, u32[]{:S(2)}) async-start(f32[8,4,128,128]{3,2,1,0:T(8,128)} %copy-done.12), calls=%async_computation.5 | async-start | bytes 4194304 | tf_op jit(solution)/shard_map/all_to_all | solution.py:369
  277.8 49.1 %copy-start.9 = (f32[8,128,128]{2,1,0:T(8,128)S(1)}, f32[8,128,128]{2,1,0:T(8,128)}, u32[]{:S(2)}) copy-start(f32[8,128,128]{2,1,0:T(8,128)} %copy-done.8) | copy-start | bytes 1572868
  277.8 49.1 %copy-start.22 = (f32[8,2,128,128]{3,2,1,0:T(8,128)S(1)}, f32[8,2,128,128]{3,2,1,0:T(8,128)}, u32[]{:S(2)}) copy-start(f32[8,2,128,128]{3,2,1,0:T(8,128)} %copy-done.21) | copy-start | bytes 3145732
  325.4 15.0 %collective-permute-start.7 = (f32[8,2,128,128]{3,2,1,0:T(8,128)S(1)}, f32[8,2,128,128]{3,2,1,0:T(8,128)S(1)}, u32[]{:S(2)}, u32[]{:S(2)}) collective-permute-start(f32[8,2,128,128]{3,2,1,0:T(8,128)S(1)} %kerr_chunk.6.refs_0_), channel_id=1, source_target_pairs={{8,0},{24,16},{9,1},{25,17},{10,2},{26,18},{11,3},{27,19},{12,4},{... | collective-permute-start | bytes 3145736 | tf_op jit(solution)/shard_map/ppermute | solution.py:372
  340.7 58.9 %collective-permute-start.8 = (f32[8,2,128,128]{3,2,1,0:T(8,128)S(1)}, f32[8,2,128,128]{3,2,1,0:T(8,128)}, u32[]{:S(2)}, u32[]{:S(2)}) collective-permute-start(f32[8,2,128,128]{3,2,1,0:T(8,128)S(1)} %carry.16.refs_0_), channel_id=1, source_target_pairs={{16,0},{17,1},{18,2},{19,3},{20,4},{21,5},{22,6},{23,7}} | collective-permute-start | bytes 3145736 | tf_op jit(solution)/shard_map/ppermute | solution.py:375
  342.0 69.2 %all-to-all-start.2 = ((f32[8,4,128,128]{3,2,1,0:T(8,128)}), f32[8,4,128,128]{3,2,1,0:T(8,128)}, u32[]{:S(2)}, u32[]{:S(2)}) async-start(f32[8,4,128,128]{3,2,1,0:T(8,128)} %carry.15.refs_1_), calls=%async_computation.2 | async-start | bytes 4194304 | tf_op jit(solution)/shard_map/all_to_all | solution.py:369
  398.3 4.7 collective-permute-start.10
  399.6 8.8 %collective-permute-start.9 = (f32[8,2,128,128]{3,2,1,0:T(8,128)}, f32[8,2,128,128]{3,2,1,0:T(8,128)S(1)}, u32[]{:S(2)}, u32[]{:S(2)}) collective-permute-start(f32[8,2,128,128]{3,2,1,0:T(8,128)} %collective-permute-done.8.refs_1_), channel_id=1, source_target_pairs={{0,8},{16,24},{1,9},{17,25},{2,10},{18,26},{3,11},{19,27},{4,12},{... | collective-permute-start | bytes 3145736 | tf_op jit(solution)/shard_map/ppermute | solution.py:377
  403.2 17.6 %collective-permute-start.11 = (f32[8,2,128,128]{3,2,1,0:T(8,128)S(1)}, f32[8,2,128,128]{3,2,1,0:T(8,128)}, u32[]{:S(2)}, u32[]{:S(2)}) collective-permute-start(f32[8,2,128,128]{3,2,1,0:T(8,128)S(1)} %carry.19.refs_0_), channel_id=1, source_target_pairs={{16,0},{17,1},{18,2},{19,3},{20,4},{21,5},{22,6},{23,7}} | collective-permute-start | bytes 3145736 | tf_op jit(solution)/shard_map/ppermute | solution.py:375
  411.2 32.4 %all-to-all-start.4 = ((f32[8,2,128,128]{3,2,1,0:T(8,128)}), f32[8,2,128,128]{3,2,1,0:T(8,128)}, u32[]{:S(2)}, u32[]{:S(2)}) async-start(f32[8,2,128,128]{3,2,1,0:T(8,128)} %carry.18), calls=%async_computation.4 | async-start | bytes 2097152 | tf_op jit(solution)/shard_map/all_to_all | solution.py:369
  420.9 5.3 %collective-permute-start.12 = (f32[8,2,128,128]{3,2,1,0:T(8,128)}, f32[8,2,128,128]{3,2,1,0:T(8,128)S(1)}, u32[]{:S(2)}, u32[]{:S(2)}) collective-permute-start(f32[8,2,128,128]{3,2,1,0:T(8,128)} %collective-permute-done.11.refs_1_), channel_id=1, source_target_pairs={{0,8},{16,24},{1,9},{17,25},{2,10},{18,26},{3,11},{19,27},{4,12},{... | collective-permute-start | bytes 3145736 | tf_op jit(solution)/shard_map/ppermute | solution.py:377
  426.1 47.2 %copy-start.15 = (f32[128,128,32]{1,0,2:T(8,128)S(1)}, f32[128,128,32]{1,0,2:T(8,128)}, u32[]{:S(2)}) copy-start(f32[128,128,32]{1,0,2:T(8,128)} %copy-done.14) | copy-start | bytes 6291460
  426.1 47.2 %copy-start.37 = (bf16[768,256]{1,0:T(8,128)(2,1)S(1)}, bf16[768,256]{1,0:T(8,128)(2,1)}, u32[]{:S(2)}) copy-start(bf16[768,256]{1,0:T(8,128)(2,1)} %constant.23.clone.refs_6_) | copy-start | bytes 1179652
  (41 other events, 247.0 us)
